TPU v7x, 32 devices: a whole 2x2x4 slice. The times are simulated.
32 devices in a mesh: sib: 2 (over core), row: 4 (over z), col: 4 (over y, x).
Axes of the slice: x: 2, y: 2, z: 4, core: 2. Of those that a mesh axis runs over, the one named last changes fastest.
Arguments:
- front_inverse: bfloat16 [24576, 24576], P('row', 'col'), may hold values from -0.078125 to 0.078125
- panel: bfloat16 [2, 12288, 256], P('sib', 'col'), may hold values from -0.59765625 to 0.59765625
- row_map: int32 [2, 12288], P('sib'), may hold values from 0 to 24575, as said below
- diag_inverse: float32 [2, 256, 256], P('sib'), may hold values from -6 to 6
Outputs:
- offdiag_block: float32 [2, 24576, 256], P('sib', ('row', 'col'))
- diag_block: float32 [2, 256, 256], P('sib')
Inputs may be any that keep to these rules, and one draw needn't show every extreme that they name: Each row of row_map names 12288 different front rows in increasing order, the first 0 and the last 24575.
All inputs are finite; a program needn't handle non-finite values.
Results may differ from a plain program's by a relative error of at most 0.0003.
Values may be sent and summed in bfloat16 or wider, within the bound.
No kernel may reach another device: no remote copies, remote signals or barrier semaphores. Data moves between devices by JAX's collectives and lax.ppermute only.
A program may use at most 128 MiB of HBM per device.

v0:
```python
import math

import jax
import jax.numpy as jnp
from jax import lax
from jax.sharding import PartitionSpec as P


def spread_range(padded_rows, padded_places, places, lower, count):
    blk = math.gcd(count, 128)
    nblk = count // blk
    starts = lower + jnp.arange(nblk, dtype=jnp.int32) * blk
    first = jnp.searchsorted(places, starts)

    def window(begin):
        rows = lax.dynamic_slice_in_dim(padded_rows, begin, blk, 0)
        marks = lax.dynamic_slice_in_dim(padded_places, begin, blk, 0)
        return (rows, marks)

    rows, marks = jax.vmap(window)(first)
    target = starts[:, None] + jnp.arange(blk, dtype=jnp.int32)[None, :]
    onehot = marks[:, None, :] == target[:, :, None]
    table = onehot.astype(jnp.bfloat16)
    spread = jnp.einsum("njk,nkw->njw", table, rows, preferred_element_type=jnp.float32)
    hits = jnp.sum(onehot.astype(jnp.float32), axis=2)
    return (spread.astype(jnp.bfloat16).reshape(count, rows.shape[2]), hits.reshape(count))


def shards(front_inverse, panel, row_map, diag_inverse):
    row_index = lax.axis_index("row")
    col_index = lax.axis_index("col")
    ncol = lax.axis_size("col")
    front_rows, front_cols = front_inverse.shape
    share = front_rows // ncol
    width = panel.shape[2]
    col_lower = col_index * front_cols
    row_lower = row_index * front_rows
    share_lower = row_lower + col_index * share
    places_all = row_map[0]
    whole_panel = lax.all_gather(panel, "col", axis=1, tiled=True)[0]
    padded_rows = jnp.concatenate([whole_panel, jnp.zeros((128, width), jnp.bfloat16)], axis=0)
    total_front = front_rows * lax.axis_size("row")
    padded_places = jnp.concatenate([places_all, jnp.full((128,), total_front, jnp.int32)], axis=0)
    spread_cols, unused_hits = spread_range(
        padded_rows, padded_places, places_all, col_lower, front_cols
    )
    spread_rows, share_hits = spread_range(
        padded_rows, padded_places, places_all, share_lower, share
    )
    product = lax.psum_scatter(
        jnp.dot(front_inverse, spread_cols, preferred_element_type=jnp.float32),
        "col",
        scatter_dimension=0,
        tiled=True,
    )
    local_terms = jnp.dot(
        spread_rows.astype(jnp.float32).T, product, precision=lax.Precision.HIGHEST
    )
    diag_terms = lax.psum(local_terms, ("row", "col"))
    offdiag = jnp.where(share_hits[:, None] > 0.5, -product, jnp.zeros_like(product))
    diag = diag_inverse[0] + diag_terms
    return (offdiag[None], diag[None])


def solution(mesh):
    return jax.shard_map(
        shards,
        mesh=mesh,
        in_specs=(P("row", "col"), P("sib", "col", None), P("sib", None), P("sib", None, None)),
        out_specs=(P("sib", ("row", "col"), None), P("sib", None, None)),
        check_vma=False,
    )
```

profile of v0, /device:TPU:0, one launch (start us, length us, event | category | flops | bytes accessed | tf_op | source)
XLA Modules:
  0.0 446.4 jit_solution(17877992332992152850)
XLA Ops:
  8.0 22.9 %while.57 = (s32[]{:T(128)}, u32[48]{0:T(128)S(1)}, u32[48]{0:T(128)S(1)}, s32[12288]{0:T(1024)}, s32[]{:T(128)}, /*index=5*/s32[]{:T(128)}, s32[]{:T(128)}, s32[]{}) while((s32[]{:T(128)}, u32[48]{0:T(128)S(1)}, u32[48]{0:T(128)S(1)}, s32[12288]{0:T(1024)}, s32[]{:T(128)}, /*index=5*/s32[]{:T(128)}, s32[]{:T(128)}, s32[]{}) %tuple.135), condition=%wide.region_4.5_spmd.clone, body=%wide.region_3.4_spmd.clone.sunk | while | flops 1748 | bytes 6512 | solution.py:13
  31.9 70.0 %while.53 = (s32[]{:T(128)}, s32[12416]{0:T(1024)S(1)}, s32[48,1]{0,1:T(1,128)S(1)}, s32[48,128]{1,0:T(8,128)S(1)}, s32[]{:T(128)}, /*index=5*/s32[]{:T(128)}) while((s32[]{:T(128)}, s32[12416]{0:T(1024)S(1)}, s32[48,1]{0,1:T(1,128)S(1)}, s32[48,128]{1,0:T(8,128)S(1)}, s32[]{:T(128)}, /*index=5*/s32[]{:T(128)}) %tuple.117), condition=%wide.while_cond.1, body=%wide.while_body.1.sunk | while | flops 2 | bytes 2137 | solution.py:17
  101.9 6.5 %concatenate.13 = bf16[12416,256]{1,0:T(8,128)(2,1)} pad(bf16[12288,256]{1,0:T(8,128)(2,1)} %bitcast.55, bf16[]{:T(256)} %constant.88.clone.1), padding=0_128x0_0 | pad | bytes 12648450 | tf_op jit(solution)/shard_map/concatenate | solution.py:41
  108.4 109.6 %while.54 = (s32[]{:T(128)}, bf16[12416,256]{1,0:T(8,128)(2,1)}, s32[48,2]{0,1:T(2,128)S(1)}, bf16[48,128,256]{2,1,0:T(8,128)(2,1)S(1)}, s32[]{:T(128)}) while((s32[]{:T(128)}, bf16[12416,256]{1,0:T(8,128)(2,1)}, s32[48,2]{0,1:T(2,128)S(1)}, bf16[48,128,256]{2,1,0:T(8,128)(2,1)S(1)}, s32[]{:T(128)}) %tuple.114), condition=%wide.while_cond.2, body=%wide.while_body.2.sunk | while | flops 2 | bytes 131169 | solution.py:16
  109.0 1.6 bitcast_dynamic-update-slice_fusion.4
  111.3 1.6 bitcast_dynamic-update-slice_fusion.4
  113.6 1.6 bitcast_dynamic-update-slice_fusion.4
  115.9 1.6 bitcast_dynamic-update-slice_fusion.4
  118.2 1.6 bitcast_dynamic-update-slice_fusion.4
  120.4 1.6 bitcast_dynamic-update-slice_fusion.4
  122.7 1.6 bitcast_dynamic-update-slice_fusion.4
  125.0 1.6 bitcast_dynamic-update-slice_fusion.4
  127.3 1.6 bitcast_dynamic-update-slice_fusion.4
  129.6 1.6 bitcast_dynamic-update-slice_fusion.4
  131.9 1.6 bitcast_dynamic-update-slice_fusion.4
  134.1 1.6 bitcast_dynamic-update-slice_fusion.4
  136.4 1.6 bitcast_dynamic-update-slice_fusion.4
  138.7 1.6 bitcast_dynamic-update-slice_fusion.4
  141.0 1.6 bitcast_dynamic-update-slice_fusion.4
  143.3 1.6 bitcast_dynamic-update-slice_fusion.4
  145.6 1.6 bitcast_dynamic-update-slice_fusion.4
  147.8 1.6 bitcast_dynamic-update-slice_fusion.4
  150.1 1.6 bitcast_dynamic-update-slice_fusion.4
  152.4 1.6 bitcast_dynamic-update-slice_fusion.4
  154.7 1.6 bitcast_dynamic-update-slice_fusion.4
  157.0 1.6 bitcast_dynamic-update-slice_fusion.4
  159.3 1.6 bitcast_dynamic-update-slice_fusion.4
  161.5 1.6 bitcast_dynamic-update-slice_fusion.4
  163.8 1.6 bitcast_dynamic-update-slice_fusion.4
  166.1 1.6 bitcast_dynamic-update-slice_fusion.4
  168.4 1.6 bitcast_dynamic-update-slice_fusion.4
  170.7 1.6 bitcast_dynamic-update-slice_fusion.4
  173.0 1.6 bitcast_dynamic-update-slice_fusion.4
  175.2 1.6 bitcast_dynamic-update-slice_fusion.4
  177.5 1.6 bitcast_dynamic-update-slice_fusion.4
  179.8 1.6 bitcast_dynamic-update-slice_fusion.4
  182.1 1.6 bitcast_dynamic-update-slice_fusion.4
  202.6 1.6 bitcast_dynamic-update-slice_fusion.4
  217.9 3.1 fusion.10
  221.1 31.5 %convolution_bitcast_fusion = f32[6144,256]{0,1:T(8,128)} fusion(bf16[6144,256]{1,0:T(8,128)(2,1)} %bitcast.56, bf16[6144,6144]{1,0:T(8,128)(2,1)} %param.8), kind=kOutput, calls=%fused_computation.26 | convolution fusion | flops 19327352832 | bytes 84934656 | tf_op jit(solution)/shard_map/dot_general | solution.py:51
  253.3 10.0 %while.56 = (s32[]{:T(128)}, u32[12]{0:T(128)S(1)}, u32[12]{0:T(128)S(1)}, s32[12288]{0:T(1024)S(1)}, s32[]{:T(128)}, /*index=5*/s32[]{:T(128)}, s32[]{:T(128)}, s32[]{}) while((s32[]{:T(128)}, u32[12]{0:T(128)S(1)}, u32[12]{0:T(128)S(1)}, s32[12288]{0:T(1024)S(1)}, s32[]{:T(128)}, /*index=5*/s32[]{:T(128)}, s32[]{:T(128)}, ...), condition=%wide.region_1.2_spmd.clone, body=%wide.region_0.1_spmd.clone.sunk | while | flops 1208 | bytes 4784 | solution.py:13
  263.5 17.5 %while.52 = (s32[]{:T(128)}, s32[12416]{0:T(1024)S(1)}, s32[12,1]{0,1:T(1,128)S(1)}, s32[12,128]{1,0:T(8,128)S(1)}, s32[]{:T(128)}, /*index=5*/s32[]{:T(128)}) while((s32[]{:T(128)}, s32[12416]{0:T(1024)S(1)}, s32[12,1]{0,1:T(1,128)S(1)}, s32[12,128]{1,0:T(8,128)S(1)}, s32[]{:T(128)}, /*index=5*/s32[]{:T(128)}) %tuple.139), condition=%wide.while_cond, body=%wide.while_body.sunk | while | flops 2 | bytes 2137 | solution.py:17
  281.4 26.0 %while.55 = (s32[]{:T(128)}, bf16[12416,256]{1,0:T(8,128)(2,1)}, s32[12,2]{0,1:T(2,128)S(1)}, bf16[12,128,256]{2,1,0:T(8,128)(2,1)S(1)}, s32[]{:T(128)}) while((s32[]{:T(128)}, bf16[12416,256]{1,0:T(8,128)(2,1)}, s32[12,2]{0,1:T(2,128)S(1)}, bf16[12,128,256]{2,1,0:T(8,128)(2,1)S(1)}, s32[]{:T(128)}) %tuple.138), condition=%wide.while_cond.3, body=%wide.while_body.3.sunk | while | flops 2 | bytes 131169 | solution.py:16
  307.8 17.8 %reduce-scatter.2.cloned.1.call-done = f32[1536,256]{0,1:T(8,128)} async-done(((f32[6144,256]{0,1:T(8,128)}), f32[1536,256]{0,1:T(8,128)}) %reduce-scatter.2.cloned.1.call-update) | async-done | bytes 1572880 | tf_op jit(solution)/shard_map/reduce_scatter | solution.py:50
  325.6 3.3 fusion.22
  329.2 1.6 copy.7
  330.8 107.4 %all-reduce.6.cloned.1.call-done = f32[256,256]{1,0:T(8,128)} async-done(((f32[256,256]{1,0:T(8,128)}), f32[256,256]{1,0:T(8,128)}) %all-reduce.6.cloned.1.call-update) | async-done | bytes 262160 | tf_op jit(solution)/shard_map/psum | solution.py:59
  438.2 1.7 fusion.19
  (474 shorter events, 203.2 us)
Async XLA Ops:
  7.2 94.7 %all-gather.2.cloned.1.call-start = ((), (), s32[]{:S(2)}) async-start(), calls=%async_computation.1 | async-start | bytes 7864320 | tf_op jit(solution)/shard_map/all_gather | solution.py:40
  7.9 317.7 %reduce-scatter.2.cloned.1.call-start = ((), (), s32[]{:S(2)}) async-start(), calls=%async_computation.2 | async-start | bytes 7864320 | tf_op jit(solution)/shard_map/reduce_scatter | solution.py:50
  252.5 0.8 copy-start
  252.5 28.9 %copy-start.2 = (bf16[12,128,256]{2,1,0:T(8,128)(2,1)S(1)}, bf16[12,128,256]{2,1,0:T(8,128)(2,1)}, u32[]{:S(2)}) copy-start(bf16[12,128,256]{2,1,0:T(8,128)(2,1)} %custom-call.11) | copy-start | bytes 2359300
  252.6 185.6 %all-reduce.6.cloned.1.call-start = ((), (), s32[]{:S(2)}) async-start(), calls=%async_computation.3 | async-start | bytes 524288 | tf_op jit(solution)/shard_map/psum | solution.py:59
  325.6 3.4 copy-start.1
  329.0 109.2 %copy-start.3 = (f32[1,256,256]{2,1,0:T(8,128)S(1)}, f32[1,256,256]{2,1,0:T(8,128)}, u32[]{:S(2)}) copy-start(f32[1,256,256]{2,1,0:T(8,128)} %param.11) | copy-start | bytes 786436
Sparse Core Ops, SparseCore 0:
  9.8 72.8 all-gather.1
  252.7 72.8 reduce-scatter.1
  331.4 106.6 all-reduce.5
where the time goes:
time: 451 us; the launch traced here: 446 us
  local copies, waits for them, and re-layouts  263 us (58%)
  waiting for transfers between devices  126 us (28%)
  matrix products  38.3 us (8%)
  between operations  13.9 us (3%)
    gather x360, local copies, waits for them, and re-layouts  222 us
    psum x1, waiting for transfers between devices, shards(): diag_terms = lax.psum(local_terms, ('row', 'col'))  107 us
    dot_general x1, matrix products, shards(): jnp.dot(front_inverse, spread_cols, preferred_element_type=jnp.float32)  31.5 us
    gather x28, local copies, waits for them, and re-layouts, spread_range(): first = jnp.searchsorted(places, starts)  31.3 us
    reduce_scatter x1, waiting for transfers between devices, shards(): lax.psum_scatter(jnp.dot(front_inverse, spread_cols, preferred_element_ty...  17.8 us
  transfers between devices with their start and end apart: 3, of which 2 were waited for; matrix products, arithmetic and copies ran while one was open for 33% of the time, Pallas kernels for 0%

commit v1 on v0

--- a/solution.py
+++ b/solution.py
@@ -1,9 +1,638 @@
-import math
+import functools
 
 import jax
 import jax.numpy as jnp
 from jax import lax
+from jax.experimental import pallas as pl
+from jax.experimental.pallas import tpu as pltpu
 from jax.sharding import PartitionSpec as P
+import math
+
+LANES = 128
+TILE = 256
+WINDOW = TILE + LANES
+STRIP = 2 * TILE
+SLOTS = 3
+GROUP = 64
+STEPS = 256.0
+TOP = 32766.0
+LIMIT = 40 * 1024 * 1024
+FIRST = 3
+KERNELS = 3
+GROUP_TILES = 4
+SMALL = pl.CostEstimate(flops=1000, bytes_accessed=1000, transcendentals=0)
+LAST = 2
+
+
+class Layout:
+    def __init__(self, rows, cols):
+        self.strips = cols // STRIP
+        self.col_tiles = cols // TILE
+        self.row_tiles = rows // TILE
+        self.counts = 0
+        self.lists = KERNELS
+        self.col_begins = self.lists + KERNELS * self.strips
+        self.row_begins = self.col_begins + self.col_tiles
+        self.row_phases = self.row_begins + self.row_tiles
+        self.me = self.row_phases + self.row_tiles
+        self.col_base = self.me + 1
+        self.row_base = self.me + 2
+        self.size = self.me + 3
+
+
+def near_half(shard):
+    return 1 - lax.rem(shard, 2)
+
+
+def arrival(block, me):
+    shard = lax.div(block, 2)
+    near = lax.rem(block, 2) == near_half(shard)
+    away = shard ^ me
+    first = (away != 3) & (near == (away == 1))
+    return jnp.where(away == 0, 0, jnp.where(first, 1, 2))
+
+
+def plan_kernel(at, half, total_rows, before, place, own, plan, near, far, kept, sems):
+    me = place[0]
+    arriving = pltpu.make_async_copy(own, kept, sems.at[0])
+    arriving.start()
+    copies = []
+    for n, (which, out) in enumerate(((near_half(me), near), (1 - near_half(me), far))):
+        source = kept.at[pl.ds(pl.multiple_of(which * half, LANES), half)]
+        copies.append(pltpu.make_async_copy(source, out, sems.at[n + 1]))
+
+    def phase(first, last):
+        start = arrival(lax.div(first, half), me)
+        end = arrival(lax.div(last - 1, half), me)
+        return jnp.maximum(start, end)
+
+    def begin(first):
+        return jnp.minimum(lax.div(first, LANES) * LANES, total_rows - WINDOW)
+
+    for i in range(KERNELS * at.strips):
+        plan[at.lists + i] = 0
+    counts = [jnp.int32(0)] * KERNELS
+    per = STRIP // TILE
+    for s in range(at.strips):
+        first, last = before[s * per], before[(s + 1) * per]
+        when = phase(first, last)
+        some = last > first
+        taken = jnp.bool_(False)
+        for j in range(KERNELS):
+            fits = some & (when <= j) & ~taken
+            if j == 0:
+                fits = fits & (counts[j] < FIRST)
+
+            @pl.when(fits)
+            def _():
+                plan[at.lists + j * at.strips + counts[j]] = s
+
+            counts[j] = counts[j] + jnp.where(fits, 1, 0)
+            taken = taken | fits
+    arriving.wait()
+    for copy in copies:
+        copy.start()
+    for j in range(KERNELS):
+        plan[at.counts + j] = counts[j]
+    for k in range(at.col_tiles):
+        plan[at.col_begins + k] = begin(before[k])
+    base = at.col_tiles + 1
+    for k in range(at.row_tiles):
+        first, last = before[base + k], before[base + k + 1]
+        plan[at.row_begins + k] = begin(first)
+        plan[at.row_phases + k] = jnp.where(last > first, phase(first, last), 0)
+    for i in range(3):
+        plan[at.me + i] = place[i]
+    for copy in copies:
+        copy.wait()
+
+
+def make_plan(at, half, total_rows, before, place, own):
+    smem = pl.BlockSpec(memory_space=pltpu.SMEM)
+    hbm = pl.BlockSpec(memory_space=pltpu.HBM)
+    piece = jax.ShapeDtypeStruct((half, own.shape[1]), own.dtype)
+    return pl.pallas_call(
+        functools.partial(plan_kernel, at, half, total_rows),
+        in_specs=[smem, smem, hbm],
+        out_specs=[smem, hbm, hbm],
+        out_shape=[jax.ShapeDtypeStruct((at.size,), jnp.int32), piece, piece],
+        scratch_shapes=[pltpu.VMEM(own.shape, own.dtype), pltpu.SemaphoreType.DMA((3,))],
+        compiler_params=pltpu.CompilerParams(vmem_limit_bytes=LIMIT),
+        cost_estimate=SMALL,
+        name="plan",
+    )(before, place, own)
+
+
+def window_hits(map_ref, begin, target):
+    first = lax.div(begin, LANES)
+    row = jnp.concatenate([map_ref[first + j] for j in range(WINDOW // LANES)], axis=1)
+    wanted = lax.broadcasted_iota(jnp.int32, (TILE, WINDOW), 0) + target
+    return wanted == row
+
+
+def spread_tile(panel_ref, map_ref, begin, target):
+    table = jnp.where(window_hits(map_ref, begin, target), 1.0, 0.0).astype(jnp.bfloat16)
+    rows = panel_ref[pl.ds(pl.multiple_of(begin, LANES), WINDOW), :]
+    return jnp.dot(table, rows, preferred_element_type=jnp.float32).astype(jnp.bfloat16)
+
+
+def strip_tile(at, s, plan, map_ref, panel, strip):
+    per = STRIP // TILE
+    for t in range(per):
+        k = s * per + t
+        strip[t * TILE:(t + 1) * TILE, :] = spread_tile(
+            panel, map_ref, plan[at.col_begins + k], plan[at.col_base] + k * TILE
+        )
+
+
+def half_block(shard, near):
+    return shard * 2 + (near_half(shard) if near else 1 - near_half(shard))
+
+
+def piece_blocks(me):
+    return [
+        me,
+        half_block(me ^ 1, True), half_block(me ^ 2, False),
+        half_block(me ^ 1, False), half_block(me ^ 2, True),
+        half_block(me ^ 3, True), half_block(me ^ 3, False),
+    ]
+
+
+def load_panel(step, me, pieces, panel, sems):
+    copies = []
+    for n, (piece, block) in enumerate(zip(pieces, piece_blocks(me))):
+        size = piece.shape[0]
+        copies.append(
+            pltpu.make_async_copy(piece, panel.at[pl.ds(pl.multiple_of(block * size, LANES), size)], sems.at[n])
+        )
+    for copy in copies:
+        copy.start()
+    half = pieces[0].shape[0] // 2
+    if step < LAST:
+        for block in range(panel.shape[0] // half):
+            @pl.when(arrival(jnp.int32(block), me) > step)
+            def _():
+                panel[block * half:(block + 1) * half, :] = jnp.zeros((half, panel.shape[1]), panel.dtype)
+    for copy in copies:
+        copy.wait()
+
+
+def build_rows(at, plan, map_ref, panel, spread, group):
+    size = GROUP_TILES
+    for t in range(size):
+        k = group * size + t
+        spread[t * TILE:(t + 1) * TILE, :] = spread_tile(
+            panel, map_ref, plan[at.row_begins + k], plan[at.row_base] + k * TILE
+        )
+
+
+def fetched(at, j, plan, front, fronts, sems, i):
+    s = plan[at.lists + j * at.strips + i]
+    slot = lax.rem(i, SLOTS)
+    return pltpu.make_async_copy(
+        front.at[:, pl.ds(pl.multiple_of(s * STRIP, STRIP), STRIP)], fronts.at[slot], sems.at[slot]
+    )
+
+
+def strips_begin(at, j, plan, front, fronts, sems):
+    for i in range(SLOTS - 1):
+        @pl.when(i < plan[at.counts + j])
+        def _():
+            fetched(at, j, plan, front, fronts, sems, jnp.int32(i)).start()
+
+
+def strips_loop(at, j, plan, front, fronts, sems, map_ref, panel, strips, total):
+    count = plan[at.counts + j]
+    listed = at.lists + j * at.strips
+
+    @pl.when(count > 0)
+    def _():
+        strip_tile(at, plan[listed], plan, map_ref, panel, strips.at[0])
+
+    @pl.loop(0, count)
+    def _(i):
+        @pl.when(i + SLOTS - 1 < count)
+        def _():
+            fetched(at, j, plan, front, fronts, sems, i + SLOTS - 1).start()
+
+        now = lax.rem(i, 2)
+        following = plan[listed + jnp.minimum(i + 1, count - 1)]
+        fetched(at, j, plan, front, fronts, sems, i).wait()
+        total[...] += jnp.dot(fronts[lax.rem(i, SLOTS)], strips[now], preferred_element_type=jnp.float32)
+        strip_tile(at, following, plan, map_ref, panel, strips.at[1 - now])
+
+
+def first_kernel(at, plan, front, map_ref, own, out, total, fronts, panel, strips, sems, own_sems):
+    strips_begin(at, 0, plan, front, fronts, sems)
+    load_panel(0, plan[at.me], [own], panel, own_sems)
+    total[...] = jnp.zeros_like(total)
+    strips_loop(at, 0, plan, front, fronts, sems, map_ref, panel, strips, total)
+    copy = pltpu.make_async_copy(total, out, own_sems.at[0])
+    copy.start()
+    copy.wait()
+
+
+def next_kernel(at, n_pieces, *refs):
+    plan, front, map_ref = refs[:3]
+    pieces = refs[3:3 + n_pieces]
+    start, total, spread, group_rows, fronts, panel, strips, sems, own_sems = refs[3 + n_pieces:]
+    copy = pltpu.make_async_copy(start, total, own_sems.at[n_pieces])
+    copy.start()
+    strips_begin(at, 1, plan, front, fronts, sems)
+    load_panel(1, plan[at.me], pieces, panel, own_sems)
+    copy.wait()
+    strips_loop(at, 1, plan, front, fronts, sems, map_ref, panel, strips, total)
+    size = GROUP_TILES * TILE
+
+    def written(group):
+        slot = lax.rem(group, 2)
+        return pltpu.make_async_copy(
+            group_rows.at[slot], spread.at[pl.ds(pl.multiple_of(group * size, size), size)], own_sems.at[slot]
+        )
+
+    groups = at.row_tiles // GROUP_TILES
+
+    @pl.loop(0, groups)
+    def _(group):
+        @pl.when(group >= 2)
+        def _():
+            written(group - 2).wait()
+
+        build_rows(at, plan, map_ref, panel, group_rows.at[lax.rem(group, 2)], group)
+        written(group).start()
+
+    for group in range(max(groups - 2, 0), groups):
+        written(jnp.int32(group)).wait()
+
+
+def strips_call(kernel, at, plan, front, map3, others, out_specs, out_shape, scratch, expected, name):
+    rows = front.shape[0]
+    width = others[0].shape[1]
+    vmem = pl.BlockSpec(memory_space=pltpu.VMEM)
+    smem = pl.BlockSpec(memory_space=pltpu.SMEM)
+    hbm = pl.BlockSpec(memory_space=pltpu.HBM)
+    return pl.pallas_call(
+        functools.partial(kernel, at),
+        in_specs=[smem, hbm, vmem] + [hbm] * len(others),
+        out_specs=out_specs,
+        scratch_shapes=scratch + [
+            pltpu.VMEM((SLOTS, rows, STRIP), jnp.bfloat16),
+            pltpu.VMEM((map3.shape[0] * LANES, width), jnp.bfloat16),
+            pltpu.VMEM((2, STRIP, width), jnp.bfloat16),
+            pltpu.SemaphoreType.DMA((SLOTS,)),
+            pltpu.SemaphoreType.DMA((max(len(others), 2),)),
+        ],
+        out_shape=out_shape,
+        compiler_params=pltpu.CompilerParams(vmem_limit_bytes=LIMIT),
+        cost_estimate=pl.CostEstimate(
+            flops=8 * rows * STRIP * width * expected, bytes_accessed=8 * rows * STRIP * expected, transcendentals=0
+        ),
+        name=name,
+    )(plan, front, map3, *others)
+
+
+def first_strips(at, plan, front, map3, own):
+    shape = front.shape[0], own.shape[1]
+    return strips_call(
+        first_kernel, at, plan, front, map3, [own], pl.BlockSpec(memory_space=pltpu.HBM), pltpu.HBM(shape, jnp.float32),
+        [pltpu.VMEM(shape, jnp.float32)], FIRST, "first_strips",
+    )
+
+
+def next_strips(at, plan, front, map3, pieces, start):
+    rows, width = start.shape
+    return strips_call(
+        lambda at, *refs: next_kernel(at, len(pieces), *refs), at, plan, front, map3, pieces + [start],
+        [pl.BlockSpec(memory_space=pltpu.VMEM), pl.BlockSpec(memory_space=pltpu.HBM)],
+        [pltpu.VMEM(start.shape, start.dtype), pltpu.HBM((rows, width), jnp.bfloat16)],
+        [pltpu.VMEM((2, GROUP_TILES * TILE, width), jnp.bfloat16)], at.strips, "next_strips",
+    )
+
+
+def quantized(values, out_ref):
+    rows, width = values.shape[0], values.shape[1]
+    codes = []
+    for g in range(rows // GROUP):
+        part = values[g * GROUP:(g + 1) * GROUP, :]
+        most = jnp.max(jnp.abs(part), axis=0, keepdims=True)
+        code = jnp.clip(jnp.ceil(jnp.log2(jnp.maximum(most, 1e-30)) * STEPS) + 1.0, -32000.0, 32000.0)
+        inverse = TOP / jnp.exp2(code * (1.0 / STEPS))
+        whole = jnp.clip(jnp.round(part * inverse), -TOP, TOP).astype(jnp.int32)
+        out_ref[g * GROUP:(g + 1) * GROUP, :] = whole.astype(jnp.int16)
+        codes.append(code)
+    codes.append(jnp.zeros((out_ref.shape[0] - rows - len(codes), width), jnp.float32))
+    tail = jnp.concatenate(codes, axis=0).astype(jnp.int32)
+    out_ref[rows:, :] = tail.astype(jnp.int16)
+
+
+def coded_rows(rows):
+    return rows + (rows // GROUP + 15) // 16 * 16
+
+
+def decoded(ref, rows):
+    codes = ref[rows:, :].astype(jnp.int32).astype(jnp.float32)
+    scales = jnp.exp2(codes * (1.0 / STEPS)) * (1.0 / TOP)
+    parts = []
+    for g in range(rows // GROUP):
+        part = ref[g * GROUP:(g + 1) * GROUP, :].astype(jnp.int32).astype(jnp.float32)
+        parts.append(part * scales[g:g + 1, :])
+    return jnp.concatenate(parts, axis=0)
+
+
+def part_of(total, which, part):
+    half = total.shape[0] // 8
+    return total[pl.ds(pl.multiple_of((which * 2 + part) * half, half), half), :]
+
+
+def last_strips_kernel(at, n_pieces, *refs):
+    plan, front, map_ref = refs[:3]
+    pieces = refs[3:3 + n_pieces]
+    total, x_out, y_out, written, fronts, panel, strips, sems, own_sems = refs[4 + n_pieces:]
+    me = plan[at.me]
+    j = KERNELS - 1
+
+    @pl.when(plan[at.counts + j] > 0)
+    def _():
+        strips_begin(at, j, plan, front, fronts, sems)
+        load_panel(LAST, me, pieces, panel, own_sems)
+        strips_loop(at, j, plan, front, fronts, sems, map_ref, panel, strips, total)
+
+    coded = x_out.shape[0] // 2
+    copy = pltpu.make_async_copy(total, written, own_sems.at[0])
+    copy.start()
+    quantized(part_of(total, me ^ 3, 0), x_out.at[:coded])
+    quantized(part_of(total, me ^ 1, 0), x_out.at[coded:])
+    quantized(part_of(total, me ^ 3, 1), y_out.at[:coded])
+    quantized(part_of(total, me ^ 2, 1), y_out.at[coded:])
+    copy.wait()
+
+
+def last_strips(at, plan, front, map3, pieces, total):
+    rows, width = total.shape
+    coded = coded_rows(rows // 8)
+    vmem = pl.BlockSpec(memory_space=pltpu.VMEM)
+    smem = pl.BlockSpec(memory_space=pltpu.SMEM)
+    hbm = pl.BlockSpec(memory_space=pltpu.HBM)
+    return pl.pallas_call(
+        functools.partial(last_strips_kernel, at, len(pieces)),
+        in_specs=[smem, hbm, vmem] + [hbm] * len(pieces) + [vmem],
+        out_specs=[vmem, vmem, vmem, hbm],
+        scratch_shapes=[
+            pltpu.VMEM((SLOTS, rows, STRIP), jnp.bfloat16),
+            pltpu.VMEM((map3.shape[0] * LANES, width), jnp.bfloat16),
+            pltpu.VMEM((2, STRIP, width), jnp.bfloat16),
+            pltpu.SemaphoreType.DMA((SLOTS,)),
+            pltpu.SemaphoreType.DMA((len(pieces),)),
+        ],
+        out_shape=[
+            pltpu.VMEM(total.shape, total.dtype),
+            jax.ShapeDtypeStruct((2 * coded, width), jnp.int16),
+            jax.ShapeDtypeStruct((2 * coded, width), jnp.int16),
+            pltpu.HBM(total.shape, total.dtype),
+        ],
+        input_output_aliases={3 + len(pieces): 0},
+        compiler_params=pltpu.CompilerParams(vmem_limit_bytes=LIMIT),
+        cost_estimate=SMALL,
+        name="last_strips",
+    )(plan, front, map3, *pieces, total)[1:]
+
+
+def diag_kernel(at, n_pieces, *refs):
+    plan, total_ref, early, map_ref = refs[:4]
+    pieces = refs[4:4 + n_pieces]
+    out, left, panel, sems = refs[4 + n_pieces:]
+    step = pl.program_id(0)
+
+    def latest(first, n):
+        late = plan[at.row_phases + first]
+        for k in range(1, n):
+            late = jnp.maximum(late, plan[at.row_phases + first + k])
+        return late
+
+    @pl.when(step == 0)
+    def _():
+        out[...] = jnp.zeros_like(out)
+
+        @pl.when(latest(0, at.row_tiles) == LAST)
+        def _():
+            load_panel(LAST, plan[at.me], pieces, panel, sems)
+
+    late = latest(step * GROUP_TILES, GROUP_TILES) == LAST
+
+    @pl.when(late)
+    def _():
+        build_rows(at, plan, map_ref, panel, left, step)
+
+    @pl.when(~late)
+    def _():
+        left[...] = early[...]
+
+    across = (((0,), (0,)), ((), ()))
+    values = total_ref[...]
+    high = values.astype(jnp.bfloat16)
+    low = (values - high.astype(jnp.float32)).astype(jnp.bfloat16)
+    out[...] += lax.dot_general(left[...], high, across, preferred_element_type=jnp.float32) + lax.dot_general(
+        left[...], low, across, preferred_element_type=jnp.float32
+    )
+
+
+def diag_product(at, plan, map3, pieces, early, total):
+    rows, width = total.shape
+    chunk = GROUP_TILES * TILE
+    vmem = pl.BlockSpec(memory_space=pltpu.VMEM)
+    hbm = pl.BlockSpec(memory_space=pltpu.HBM)
+    block = pl.BlockSpec((chunk, width), lambda i, plan: (i, 0))
+    return pl.pallas_call(
+        functools.partial(diag_kernel, at, len(pieces)),
+        grid_spec=pltpu.PrefetchScalarGridSpec(
+            num_scalar_prefetch=1,
+            grid=(rows // chunk,),
+            in_specs=[block, block, vmem] + [hbm] * len(pieces),
+            out_specs=pl.BlockSpec((width, width), lambda i, plan: (0, 0)),
+            scratch_shapes=[
+                pltpu.VMEM((chunk, width), jnp.bfloat16),
+                pltpu.VMEM((map3.shape[0] * LANES, width), jnp.bfloat16),
+                pltpu.SemaphoreType.DMA((len(pieces),)),
+            ],
+        ),
+        out_shape=jax.ShapeDtypeStruct((width, width), jnp.float32),
+        compiler_params=pltpu.CompilerParams(vmem_limit_bytes=LIMIT),
+        cost_estimate=SMALL,
+        name="diag_product",
+    )(plan, total, early, map3, *pieces)
+
+
+def second_kernel(plan, low_ref, high_ref, x_in, y_in, low_out, high_out):
+    rows = low_ref.shape[0]
+    quantized(low_ref[...] + decoded(x_in, rows), low_out)
+    quantized(high_ref[...] + decoded(y_in, rows), high_out)
+
+
+def second_hop(at, plan, total, x_in, y_in):
+    half, width = total.shape[0] // 8, total.shape[1]
+    coded = x_in.shape[0] // 2
+    payload = pl.BlockSpec((coded, width), lambda i, plan: (0, 0))
+    return pl.pallas_call(
+        second_kernel,
+        grid_spec=pltpu.PrefetchScalarGridSpec(
+            num_scalar_prefetch=1,
+            grid=(1,),
+            in_specs=[
+                pl.BlockSpec((half, width), lambda i, plan: ((plan[at.me] ^ 2) * 2, 0)),
+                pl.BlockSpec((half, width), lambda i, plan: ((plan[at.me] ^ 1) * 2 + 1, 0)),
+                payload,
+                payload,
+            ],
+            out_specs=[payload, payload],
+        ),
+        out_shape=[jax.ShapeDtypeStruct((coded, width), jnp.int16)] * 2,
+        compiler_params=pltpu.CompilerParams(vmem_limit_bytes=LIMIT),
+        cost_estimate=SMALL,
+        name="second_hop",
+    )(plan, total, total, x_in, y_in)
+
+
+def terms_kernel(n, *refs):
+    refs[-1][...] = sum((ref[...] for ref in refs[1:n]), refs[0][...])
+
+
+def added(terms, after):
+    vmem = pl.BlockSpec(memory_space=pltpu.VMEM)
+    return pl.pallas_call(
+        functools.partial(terms_kernel, len(terms)),
+        in_specs=[vmem] * len(terms) + [pl.BlockSpec(memory_space=pl.ANY)] * len(after),
+        out_specs=vmem,
+        out_shape=jax.ShapeDtypeStruct(terms[0].shape, terms[0].dtype),
+        compiler_params=pltpu.CompilerParams(vmem_limit_bytes=LIMIT),
+        cost_estimate=SMALL,
+        name="added",
+    )(*terms, *after)
+
+
+def last_kernel(at, plan, low_ref, high_ref, x_in, y_in, low_in, high_in, map_ref, out_ref):
+    me = plan[at.me]
+    rows = low_ref.shape[0]
+    tiles = rows // TILE
+    sums = [
+        low_ref[...] + decoded(x_in, rows) + decoded(low_in, rows),
+        high_ref[...] + decoded(y_in, rows) + decoded(high_in, rows),
+    ]
+    for part, value in enumerate(sums):
+        for j in range(tiles):
+            n = part * tiles + j
+            k = me * 2 * tiles + n
+            hits = window_hits(map_ref, plan[at.row_begins + k], plan[at.row_base] + k * TILE)
+            marked = jnp.max(jnp.where(hits, 1.0, 0.0), axis=1, keepdims=True)
+            tile = value[j * TILE:(j + 1) * TILE, :]
+            out_ref[n * TILE:(n + 1) * TILE, :] = jnp.where(marked > 0.5, -tile, 0.0)
+
+
+def last_sum(at, plan, total, x_in, y_in, low_in, high_in, map3):
+    half, width = total.shape[0] // 8, total.shape[1]
+    coded = low_in.shape[0]
+
+    def block(rows, n):
+        return pl.BlockSpec((rows, width), lambda i, plan: (n, 0))
+
+    return pl.pallas_call(
+        functools.partial(last_kernel, at),
+        grid_spec=pltpu.PrefetchScalarGridSpec(
+            num_scalar_prefetch=1,
+            grid=(1,),
+            in_specs=[
+                pl.BlockSpec((half, width), lambda i, plan: (plan[at.me] * 2, 0)),
+                pl.BlockSpec((half, width), lambda i, plan: (plan[at.me] * 2 + 1, 0)),
+                block(coded, 1), block(coded, 1), block(coded, 0), block(coded, 0),
+                pl.BlockSpec(map3.shape, lambda i, plan: (0, 0, 0)),
+            ],
+            out_specs=block(2 * half, 0),
+        ),
+        out_shape=jax.ShapeDtypeStruct((2 * half, width), jnp.float32),
+        compiler_params=pltpu.CompilerParams(vmem_limit_bytes=LIMIT),
+        cost_estimate=SMALL,
+        name="last_sum",
+    )(plan, total, total, x_in, y_in, low_in, high_in, map3)
+
+
+def shares(block, axis):
+    n = lax.axis_size(axis)
+    me = lax.axis_index(axis)
+    share = block.shape[0] // n
+
+    def shifted(value, by):
+        return lax.ppermute(value, axis, [(i, (i + by) % n) for i in range(n)])
+
+    def part(of):
+        return lax.dynamic_slice_in_dim(block, lax.rem(of, n) * share, share, 0)
+
+    arrived = [shifted(part(me + by), by) for by in range(1, n)]
+    return [part(me)] + arrived, shifted
+
+
+def spread_out(mine, shifted, axis):
+    n = lax.axis_size(axis)
+    me = lax.axis_index(axis)
+    share = mine.shape[0]
+    whole = jnp.zeros((n * share,) + mine.shape[1:], mine.dtype)
+    for by in range(n):
+        value = mine if by == 0 else shifted(mine, by)
+        whole = lax.dynamic_update_slice_in_dim(whole, value, lax.rem(me - by + n, n) * share, 0)
+    return whole
+
+
+def four_columns(front, panel, row_map, diag_inverse):
+    me = lax.axis_index("col")
+    rows, cols = front.shape
+    own = panel[0]
+    half = own.shape[0] // 2
+    places = row_map[0]
+    map3 = places.reshape(-1, 1, LANES)
+    total_rows = places.shape[0]
+    at = Layout(rows, cols)
+
+    def partner(value, bit):
+        return lax.ppermute(value, "col", [(i, i ^ bit) for i in range(4)])
+
+    def half_of(which):
+        return lax.dynamic_slice_in_dim(own, which * half, half, 0)
+
+    high = near_half(me)
+    x_near = partner(half_of(high), 1)
+    y_far = partner(half_of(1 - high), 2)
+
+    col_base = me * cols
+    row_base = lax.axis_index("row") * rows
+    marks = jnp.concatenate([
+        col_base + TILE * jnp.arange(cols // TILE + 1, dtype=jnp.int32),
+        row_base + TILE * jnp.arange(rows // TILE + 1, dtype=jnp.int32),
+    ])
+    before = jnp.sum(places[None, :] < marks[:, None], axis=1, dtype=jnp.int32)
+    place = jnp.stack([me, col_base, row_base]).astype(jnp.int32)
+    plan, near, far = make_plan(at, half, total_rows, before, place, own)
+
+    x_far = partner(far, 1)
+    y_near = partner(near, 2)
+    start = first_strips(at, plan, front, map3, own)
+    d_near = partner(x_near, 2)
+    d_far = partner(y_far, 1)
+    pieces = [own, x_near, y_far]
+    total, early = next_strips(at, plan, front, map3, pieces, start)
+    pieces += [x_far, y_near, d_near, d_far]
+    to_x, to_y, total = last_strips(at, plan, front, map3, pieces, total)
+    total = pltpu.with_memory_space_constraint(total, pltpu.HBM)
+    from_x = partner(to_x, 1)
+    from_y = partner(to_y, 2)
+    in_hbm = [pltpu.with_memory_space_constraint(piece, pltpu.HBM) for piece in pieces]
+    terms, shifted = shares(diag_product(at, plan, map3, in_hbm, early, total), "row")
+    low, high = second_hop(at, plan, total, from_x, from_y)
+    mine = sum(terms[1:], terms[0])
+    terms = [mine] + [partner(mine, bit) for bit in (1, 2, 3)]
+    mine = added(terms, [low])
+    low = partner(low, 2)
+    high = partner(high, 1)
+    diag = diag_inverse[0] + spread_out(mine, shifted, "row")
+    offdiag = last_sum(at, plan, total, from_x, from_y, low, high, map3)
+    return offdiag[None], diag[None]
 
 
 def spread_range(padded_rows, padded_places, places, lower, count):
@@ -26,7 +655,7 @@
     return (spread.astype(jnp.bfloat16).reshape(count, rows.shape[2]), hits.reshape(count))
 
 
-def shards(front_inverse, panel, row_map, diag_inverse):
+def any_columns(front_inverse, panel, row_map, diag_inverse):
     row_index = lax.axis_index("row")
     col_index = lax.axis_index("col")
     ncol = lax.axis_size("col")
@@ -64,7 +693,7 @@
 
 def solution(mesh):
     return jax.shard_map(
-        shards,
+        four_columns if mesh.shape["col"] == 4 else any_columns,
         mesh=mesh,
         in_specs=(P("row", "col"), P("sib", "col", None), P("sib", None), P("sib", None, None)),
         out_specs=(P("sib", ("row", "col"), None), P("sib", None, None)),

time: 451 us -> 120 us (0.27)
  local copies, waits for them, and re-layouts: 263 us -> 4.75 us
  waiting for transfers between devices: 126 us -> 20.3 us
  Pallas kernels: 0 us -> 54.2 us
  matrix products: 38.3 us -> 0 us
  starting transfers between devices: 0.12 us -> 38.2 us
  between operations: 13.9 us -> 0.87 us
    gather x388 -> x0, local copies, waits for them, and re-layouts: 253 us -> none
    psum x1 -> x0, waiting for transfers between devices: 107 us -> none  [shards(): diag_terms = lax.psum(local_terms, ('row', 'col'))]
    pallas_call x0 -> x8, Pallas kernels: none -> 54.2 us  [the longest x2 34.1 us: strips_call(): pl.pallas_call(functools.partial(kernel, at), in_specs=[smem, hbm, vmem]...]
    dot_general x4 -> x0, matrix products: 38.3 us -> none  [the longest x1 31.5 us: shards(): jnp.dot(front_inverse, spread_cols, preferred_element_type=jnp.float32)]
    ppermute x0 -> x19, starting transfers between devices: none -> 38.2 us  [the longest x13 23.9 us: partner(): return lax.ppermute(value, 'col', [(i, i ^ bit) for i in range(4)])]
    ppermute x0 -> x19, waiting for transfers between devices: none -> 20.3 us  [the longest x13 15.3 us: partner(): return lax.ppermute(value, 'col', [(i, i ^ bit) for i in range(4)])]
    reduce_scatter x1 -> x0, waiting for transfers between devices: 17.8 us -> none  [shards(): lax.psum_scatter(jnp.dot(front_inverse, spread_cols, preferred_element_ty...]
    concatenate x4 -> x0, local copies, waits for them, and re-layouts: 7.3 us -> none  [the longest x1 6.48 us: shards(): jnp.concatenate([whole_panel, jnp.zeros((128, width), jnp.bfloat16)], axi...]
  transfers between devices with their start and end apart: 3 -> 19, of which waited for: 2 -> 9; matrix products, arithmetic and copies ran while one was open for 33% -> 1% of each run, Pallas kernels for 0% -> 38%
where the time goes in v1:
time: 120 us
  Pallas kernels  54.2 us (45%)
  starting transfers between devices  38.2 us (32%)
  waiting for transfers between devices  20.3 us (17%)
  local copies, waits for them, and re-layouts  4.75 us (4%)
  other arithmetic  1.43 us (1%)
    pallas_call x2, Pallas kernels, strips_call(): pl.pallas_call(functools.partial(kernel, at), in_specs=[smem, hbm, vmem]...  34.1 us
    ppermute x13, starting transfers between devices, partner(): return lax.ppermute(value, 'col', [(i, i ^ bit) for i in range(4)])  23.9 us
    ppermute x13, waiting for transfers between devices, partner(): return lax.ppermute(value, 'col', [(i, i ^ bit) for i in range(4)])  15.3 us
    ppermute x6, starting transfers between devices, shifted(): return lax.ppermute(value, axis, [(i, (i + by) % n) for i in range(n)])  14.4 us
    pallas_call x1, Pallas kernels, diag_product(): pl.pallas_call(functools.partial(diag_kernel, at, len(pieces)), grid_spec...  6.64 us
    ppermute x6, waiting for transfers between devices, shifted(): return lax.ppermute(value, axis, [(i, (i + by) % n) for i in range(n)])  4.99 us
    pallas_call x1, Pallas kernels, last_strips(): pl.pallas_call(functools.partial(last_strips_kernel, at, len(pieces)), in...  4.64 us
    pallas_call x1, Pallas kernels, last_sum(): pl.pallas_call(functools.partial(last_kernel, at), grid_spec=pltpu.Prefet...  3.87 us
  transfers between devices with their start and end apart: 19, of which 9 were waited for; matrix products, arithmetic and copies ran while one was open for 1% of the time, Pallas kernels for 38%

profile of v1, /device:TPU:0, one launch (start us, length us, event | category | flops | bytes accessed | tf_op | source)
XLA Modules:
  0.0 119.8 jit_solution(3246997900181059292)
XLA Ops:
  0.6 0.0 copy-start
  0.7 2.7 %dynamic-slice_bitcast_fusion = (bf16[1536,256]{1,0:T(8,128)(2,1)}, bf16[1536,256]{1,0:T(8,128)(2,1)}) fusion(bf16[1,3072,256]{2,1,0:T(8,128)(2,1)} %param.5, s32[]{:T(128)S(6)} %select_n.25, s32[]{:T(128)S(6)} %select_n.24), kind=kLoop, calls=%fused_computation.1 | loop fusion | bytes 3145736 | tf_op jit(solution)/shard_map/dynamic_slice | solution.py:597
  3.4 2.9 %collective-permute-start = (bf16[1536,256]{1,0:T(8,128)(2,1)}, bf16[1536,256]{1,0:T(8,128)(2,1)S(1)}, u32[]{:S(2)}, u32[]{:S(2)}) collective-permute-start(bf16[1536,256]{1,0:T(8,128)(2,1)} %get-tuple-element.23), channel_id=1, source_target_pairs={{0,1},{1,0},{2,3},{3,2},{4,5},{5,4},{6,7},{7,6},{8,9},{9,8},{10,11... | collective-permute-start | bytes 2359304 | tf_op jit(solution)/shard_map/ppermute | solution.py:594
  6.3 1.5 %collective-permute-start.1 = (bf16[1536,256]{1,0:T(8,128)(2,1)}, bf16[1536,256]{1,0:T(8,128)(2,1)S(1)}, u32[]{:S(2)}, u32[]{:S(2)}) collective-permute-start(bf16[1536,256]{1,0:T(8,128)(2,1)} %get-tuple-element.22), channel_id=1, source_target_pairs={{0,2},{1,3},{2,0},{3,1},{4,6},{5,7},{6,4},{7,5},{8,10},{9,11},{10,... | collective-permute-start | bytes 2359304 | tf_op jit(solution)/shard_map/ppermute | solution.py:594
  7.9 0.1 pad_add_fusion
  7.9 0.5 convert_reduce_fusion.before
  8.5 0.1 pad_add_fusion.1.place
  8.5 2.4 %plan.1 = (s32[114]{0:T(128)S(1)}, bf16[1536,256]{1,0:T(8,128)(2,1)S(1)}, bf16[1536,256]{1,0:T(8,128)(2,1)S(1)}) custom-call(s32[50]{0:T(128)S(1)} %convert_reduce_fusion.before, s32[3]{0:T(128)S(1)} %pad_add_fusion.1.place, bf16[3072,256]{1,0:T(8,128)(2,1)S(1)} %bitcast.18), custom_call_target="tpu_custom_call" | custom-call | flops 1000 | bytes 1000 | tf_op jit(solution)/shard_map/plan/pallas_call | solution.py:114
  11.0 0.6 collective-permute-start.2
  11.6 0.1 collective-permute-start.3
  11.6 11.9 %first_strips.1.refs_6_ = f32[6144,256]{1,0:T(8,128)} custom-call(s32[114]{0:T(128)S(1)} %get-tuple-element.12.plan.refs_0_, bf16[6144,6144]{1,0:T(8,128)(2,1)} %refs_1_.3, s32[96,1,128]{2,1,0:T(1,128)S(1)} %bitcast.23, bf16[3072,256]{1,0:T(8,128)(2,1)S(1)} %bitcast.19), custom_call_target="tpu_custom_call" | custom-call | flops 19327352832 | bytes 75497472 | tf_op jit(solution)/shard_map/first_strips/pallas_call | solution.py:274
  23.5 1.4 %collective-permute-done.refs_4_.refs_5_ = bf16[1536,256]{1,0:T(8,128)(2,1)S(1)} collective-permute-done((bf16[1536,256]{1,0:T(8,128)(2,1)}, bf16[1536,256]{1,0:T(8,128)(2,1)S(1)}, u32[]{:S(2)}, u32[]{:S(2)}) %collective-permute-start) | collective-permute-done | bytes 786464 | tf_op jit(solution)/shard_map/ppermute | solution.py:594
  24.9 2.1 %collective-permute-start.4 = (bf16[1536,256]{1,0:T(8,128)(2,1)S(1)}, bf16[1536,256]{1,0:T(8,128)(2,1)S(1)}, u32[]{:S(2)}, u32[]{:S(2)}) collective-permute-start(bf16[1536,256]{1,0:T(8,128)(2,1)S(1)} %collective-permute-done.refs_4_.refs_5_), channel_id=1, source_target_pairs={{0,2},{1,3},{2,0},{3,1},{4,6},{5,7},{6,4},{7,5},{8,10},{9,11},{10,... | collective-permute-start | bytes 2359304 | tf_op jit(solution)/shard_map/ppermute | solution.py:594
  27.0 0.0 collective-permute-done.1.refs_5_.refs_6_
  27.0 1.5 %collective-permute-start.5 = (bf16[1536,256]{1,0:T(8,128)(2,1)S(1)}, bf16[1536,256]{1,0:T(8,128)(2,1)S(1)}, u32[]{:S(2)}, u32[]{:S(2)}) collective-permute-start(bf16[1536,256]{1,0:T(8,128)(2,1)S(1)} %collective-permute-done.1.refs_5_.refs_6_), channel_id=1, source_target_pairs={{0,1},{1,0},{2,3},{3,2},{4,5},{5,4},{6,7},{7,6},{8,9},{9,8},{10,11... | collective-permute-start | bytes 2359304 | tf_op jit(solution)/shard_map/ppermute | solution.py:594
  28.5 22.3 %next_strips.1 = (f32[6144,256]{1,0:T(8,128)S(1)}, bf16[6144,256]{1,0:T(8,128)(2,1)}) custom-call(s32[114]{0:T(128)S(1)} %get-tuple-element.12.plan.refs_0_, bf16[6144,6144]{1,0:T(8,128)(2,1)} %refs_1_.3, s32[96,1,128]{2,1,0:T(1,128)S(1)} %bitcast.24, bf16[3072,256]{1,0:T(8,128)(2,1)S(1)} %bitcast.20, ...), custom_call_target="tpu_custom_call" | custom-call | flops 77309411328 | bytes 301989888 | tf_op jit(solution)/shard_map/next_strips/pallas_call | solution.py:274
  50.8 0.0 collective-permute-done.2.refs_6_.refs_7_
  50.8 0.0 collective-permute-done.3.refs_7_.refs_8_
  50.8 8.4 %collective-permute-done.4.refs_8_.refs_9_ = bf16[1536,256]{1,0:T(8,128)(2,1)S(1)} collective-permute-done((bf16[1536,256]{1,0:T(8,128)(2,1)S(1)}, bf16[1536,256]{1,0:T(8,128)(2,1)S(1)}, u32[]{:S(2)}, u32[]{:S(2)}) %collective-permute-start.4) | collective-permute-done | bytes 786464 | tf_op jit(solution)/shard_map/ppermute | solution.py:594
  59.3 4.6 %last_strips.1 = (f32[6144,256]{1,0:T(8,128)S(1)}, s16[1568,256]{1,0:T(8,128)(2,1)}, s16[1568,256]{1,0:T(8,128)(2,1)}, f32[6144,256]{1,0:T(8,128)}) custom-call(s32[114]{0:T(128)S(1)} %get-tuple-element.12.plan.refs_0_, bf16[6144,6144]{1,0:T(8,128)(2,1)} %refs_1_.3, s32[96,1,128]{2,1,0:T(1,128)S(1)} %bitcast.25, ...), custom_call_target="tpu_custom_call", output_to_operand_aliasing={{0}: (10, {})} | custom-call | flops 1000 | bytes 1000 | tf_op jit(solution)/shard_map/last_strips/pallas_call | solution.py:376
  64.0 9.4 %collective-permute-start.6 = (s16[1568,256]{1,0:T(8,128)(2,1)}, s16[1568,256]{1,0:T(8,128)(2,1)S(1)}, u32[]{:S(2)}, u32[]{:S(2)}) collective-permute-start(s16[1568,256]{1,0:T(8,128)(2,1)} %get-tuple-element.17), channel_id=1, source_target_pairs={{0,1},{1,0},{2,3},{3,2},{4,5},{5,4},{6,7},{7,6},{8,9},{9,8},{10,11... | collective-permute-start | bytes 2408456 | tf_op jit(solution)/shard_map/ppermute | solution.py:594
  73.4 1.9 %copy-done.7 = bf16[6144,256]{1,0:T(8,128)(2,1)S(1)} copy-done((bf16[6144,256]{1,0:T(8,128)(2,1)S(1)}, bf16[6144,256]{1,0:T(8,128)(2,1)}, u32[]{:S(2)}) %copy-start.7) | copy-done | bytes 3145752
  75.3 6.6 %diag_product.1 = f32[256,256]{1,0:T(8,128)S(1)} custom-call(s32[114]{0:T(128)S(1)} %get-tuple-element.12.plan.refs_0_, f32[6144,256]{1,0:T(8,128)} %get-tuple-element.16.low_ref.high_ref.refs_1_, bf16[6144,256]{1,0:T(8,128)(2,1)S(1)} %copy-done.7, s32[96,1,128]{2,1,0:T(1,128)S(1)} %bitcast.26, bf16[3072,256]{1,0:T(8,128)(2,1)} %bitcast.17, ...), custom_call_target="tpu_custom_call" | custom-call | flops 1000 | bytes 1000 | tf_op jit(solution)/shard_map/diag_product/pallas_call | solution.py:445
  81.9 5.4 %collective-permute-start.10 = (f32[64,256]{1,0:T(8,128)S(1)}, f32[64,256]{1,0:T(8,128)S(1)}, u32[]{:S(2)}, u32[]{:S(2)}) collective-permute-start(f32[64,256]{1,0:T(8,128)S(1)} %get-tuple-element.24), channel_id=1, source_target_pairs={{0,4},{4,8},{8,12},{12,0},{1,5},{5,9},{9,13},{13,1},{2,6},{6,10},{... | collective-permute-start | bytes 196616 | tf_op jit(solution)/shard_map/ppermute | solution.py:563
  87.4 3.3 %collective-permute-start.11 = (f32[64,256]{1,0:T(8,128)S(1)}, f32[64,256]{1,0:T(8,128)S(1)}, u32[]{:S(2)}, u32[]{:S(2)}) collective-permute-start(f32[64,256]{1,0:T(8,128)S(1)} %get-tuple-element.26), channel_id=1, source_target_pairs={{0,8},{4,12},{8,0},{12,4},{1,9},{5,13},{9,1},{13,5},{2,10},{6,14},... | collective-permute-start | bytes 196616 | tf_op jit(solution)/shard_map/ppermute | solution.py:563
  90.7 1.4 %collective-permute-start.12 = (f32[64,256]{1,0:T(8,128)S(1)}, f32[64,256]{1,0:T(8,128)S(1)}, u32[]{:S(2)}, u32[]{:S(2)}) collective-permute-start(f32[64,256]{1,0:T(8,128)S(1)} %get-tuple-element.25), channel_id=1, source_target_pairs={{0,12},{4,0},{8,4},{12,8},{1,13},{5,1},{9,5},{13,9},{2,14},{6,2},{... | collective-permute-start | bytes 196616 | tf_op jit(solution)/shard_map/ppermute | solution.py:563
  92.1 1.0 collective-permute-done.10
  93.1 2.2 %collective-permute-done.11 = f32[64,256]{1,0:T(8,128)S(1)} collective-permute-done((f32[64,256]{1,0:T(8,128)S(1)}, f32[64,256]{1,0:T(8,128)S(1)}, u32[]{:S(2)}, u32[]{:S(2)}) %collective-permute-start.11) | collective-permute-done | bytes 65568 | tf_op jit(solution)/shard_map/ppermute | solution.py:563
  95.3 0.0 collective-permute-done.12
  95.3 0.1 collective-permute-start.13
  95.4 1.5 %collective-permute-start.14 = (f32[64,256]{1,0:T(8,128)S(1)}, f32[64,256]{1,0:T(8,128)S(1)}, u32[]{:S(2)}, u32[]{:S(2)}) collective-permute-start(f32[64,256]{1,0:T(8,128)S(1)} %add_add_fusion.refs_0_), channel_id=1, source_target_pairs={{0,2},{1,3},{2,0},{3,1},{4,6},{5,7},{6,4},{7,5},{8,10},{9,11},{10,... | collective-permute-start | bytes 196616 | tf_op jit(solution)/shard_map/ppermute | solution.py:594
  96.9 2.0 %collective-permute-start.15 = (f32[64,256]{1,0:T(8,128)S(1)}, f32[64,256]{1,0:T(8,128)S(1)}, u32[]{:S(2)}, u32[]{:S(2)}) collective-permute-start(f32[64,256]{1,0:T(8,128)S(1)} %add_add_fusion.refs_0_), channel_id=1, source_target_pairs={{0,3},{1,2},{2,1},{3,0},{4,7},{5,6},{6,5},{7,4},{8,11},{9,10},{10,... | collective-permute-start | bytes 196616 | tf_op jit(solution)/shard_map/ppermute | solution.py:594
  98.9 0.0 collective-permute-done.6.x_in
  98.9 0.0 collective-permute-done.7.y_in
  98.9 2.5 %second_hop.1 = (s16[784,256]{1,0:T(8,128)(2,1)S(1)}, s16[784,256]{1,0:T(8,128)(2,1)S(1)}) custom-call(s32[114]{0:T(128)S(1)} %get-tuple-element.12.plan.refs_0_, f32[6144,256]{1,0:T(8,128)} %get-tuple-element.16.low_ref.high_ref.refs_1_, f32[6144,256]{1,0:T(8,128)} %get-tuple-element.16.low_ref.high_ref.refs_1_, ...), custom_call_target="tpu_custom_call" | custom-call | flops 1000 | bytes 1000 | tf_op jit(solution)/shard_map/second_hop/pallas_call | solution.py:475
  101.4 0.0 collective-permute-done.13.refs_1_
  101.4 0.7 collective-permute-done.15.refs_3_
  102.1 1.8 %collective-permute-start.16 = (f32[64,256]{1,0:T(8,128)S(1)}, f32[64,256]{1,0:T(8,128)S(1)}, u32[]{:S(2)}, u32[]{:S(2)}) collective-permute-start(f32[64,256]{1,0:T(8,128)S(1)} %added.1), channel_id=1, source_target_pairs={{0,4},{4,8},{8,12},{12,0},{1,5},{5,9},{9,13},{13,1},{2,6},{6,10},{... | collective-permute-start | bytes 196616 | tf_op jit(solution)/shard_map/ppermute | solution.py:563
  103.9 1.5 %collective-permute-start.17 = (f32[64,256]{1,0:T(8,128)S(1)}, f32[64,256]{1,0:T(8,128)S(1)}, u32[]{:S(2)}, u32[]{:S(2)}) collective-permute-start(f32[64,256]{1,0:T(8,128)S(1)} %added.1), channel_id=1, source_target_pairs={{0,8},{4,12},{8,0},{12,4},{1,9},{5,13},{9,1},{13,5},{2,10},{6,14},... | collective-permute-start | bytes 196616 | tf_op jit(solution)/shard_map/ppermute | solution.py:563
  105.4 0.9 collective-permute-start.18
  106.3 0.8 collective-permute-start.8
  107.1 1.4 %collective-permute-start.9 = (s16[784,256]{1,0:T(8,128)(2,1)S(1)}, s16[784,256]{1,0:T(8,128)(2,1)S(1)}, u32[]{:S(2)}, u32[]{:S(2)}) collective-permute-start(s16[784,256]{1,0:T(8,128)(2,1)S(1)} %get-tuple-element.20), channel_id=1, source_target_pairs={{0,1},{1,0},{2,3},{3,2},{4,5},{5,4},{6,7},{7,6},{8,9},{9,8},{10,11... | collective-permute-start | bytes 1204232 | tf_op jit(solution)/shard_map/ppermute | solution.py:594
  108.6 1.4 %collective-permute-done.17 = f32[64,256]{1,0:T(8,128)S(1)} collective-permute-done((f32[64,256]{1,0:T(8,128)S(1)}, f32[64,256]{1,0:T(8,128)S(1)}, u32[]{:S(2)}, u32[]{:S(2)}) %collective-permute-start.17) | collective-permute-done | bytes 65568 | tf_op jit(solution)/shard_map/ppermute | solution.py:563
  110.0 0.4 collective-permute-done.18
  110.4 0.7 fusion
  111.1 4.1 %collective-permute-done.8.low_in = s16[784,256]{1,0:T(8,128)(2,1)S(1)} collective-permute-done((s16[784,256]{1,0:T(8,128)(2,1)S(1)}, s16[784,256]{1,0:T(8,128)(2,1)S(1)}, u32[]{:S(2)}, u32[]{:S(2)}) %collective-permute-start.8) | collective-permute-done | bytes 401440 | tf_op jit(solution)/shard_map/ppermute | solution.py:594
  115.2 0.7 collective-permute-done.9.high_in
  115.9 3.9 %last_sum.1 = f32[1536,256]{1,0:T(8,128)} custom-call(s32[114]{0:T(128)S(1)} %get-tuple-element.12.plan.refs_0_, f32[6144,256]{1,0:T(8,128)} %get-tuple-element.16.low_ref.high_ref.refs_1_, f32[6144,256]{1,0:T(8,128)} %get-tuple-element.16.low_ref.high_ref.refs_1_, s16[1568,256]{1,0:T(8,128)(2,1)S(1)} %collective-permute-done.6.x_in, ...), custom_call_target="tpu_custom_call" | custom-call | flops 1000 | bytes 1000 | tf_op jit(solution)/shard_map/last_sum/pallas_call | solution.py:537
  (31 shorter events, 0.2 us)
Async XLA Ops:
  0.6 7.9 %copy-start = (bf16[1,3072,256]{2,1,0:T(8,128)(2,1)S(1)}, bf16[1,3072,256]{2,1,0:T(8,128)(2,1)}, u32[]{:S(2)}) copy-start(bf16[1,3072,256]{2,1,0:T(8,128)(2,1)} %param.5) | copy-start | bytes 4718596
  0.6 7.3 %copy-start.8 = (s32[1,12288]{1,0:T(1,128)S(1)}, s32[1,12288]{1,0:T(1,128)}, u32[]{:S(2)}) copy-start(s32[1,12288]{1,0:T(1,128)} %param.6) | copy-start | bytes 147460
  3.4 21.5 %collective-permute-start = (bf16[1536,256]{1,0:T(8,128)(2,1)}, bf16[1536,256]{1,0:T(8,128)(2,1)S(1)}, u32[]{:S(2)}, u32[]{:S(2)}) collective-permute-start(bf16[1536,256]{1,0:T(8,128)(2,1)} %get-tuple-element.23), channel_id=1, source_target_pairs={{0,1},{1,0},{2,3},{3,2},{4,5},{5,4},{6,7},{7,6},{8,9},{9,8},{10,11... | collective-permute-start | bytes 2359304 | tf_op jit(solution)/shard_map/ppermute | solution.py:594
  6.3 20.7 %collective-permute-start.1 = (bf16[1536,256]{1,0:T(8,128)(2,1)}, bf16[1536,256]{1,0:T(8,128)(2,1)S(1)}, u32[]{:S(2)}, u32[]{:S(2)}) collective-permute-start(bf16[1536,256]{1,0:T(8,128)(2,1)} %get-tuple-element.22), channel_id=1, source_target_pairs={{0,2},{1,3},{2,0},{3,1},{4,6},{5,7},{6,4},{7,5},{8,10},{9,11},{10,... | collective-permute-start | bytes 2359304 | tf_op jit(solution)/shard_map/ppermute | solution.py:594
  11.0 39.8 %collective-permute-start.2 = (bf16[1536,256]{1,0:T(8,128)(2,1)S(1)}, bf16[1536,256]{1,0:T(8,128)(2,1)S(1)}, u32[]{:S(2)}, u32[]{:S(2)}) collective-permute-start(bf16[1536,256]{1,0:T(8,128)(2,1)S(1)} %get-tuple-element.13), channel_id=1, source_target_pairs={{0,1},{1,0},{2,3},{3,2},{4,5},{5,4},{6,7},{7,6},{8,9},{9,8},{10,11... | collective-permute-start | bytes 2359304 | tf_op jit(solution)/shard_map/ppermute | solution.py:594
  11.6 39.2 %collective-permute-start.3 = (bf16[1536,256]{1,0:T(8,128)(2,1)S(1)}, bf16[1536,256]{1,0:T(8,128)(2,1)S(1)}, u32[]{:S(2)}, u32[]{:S(2)}) collective-permute-start(bf16[1536,256]{1,0:T(8,128)(2,1)S(1)} %get-tuple-element.14), channel_id=1, source_target_pairs={{0,2},{1,3},{2,0},{3,1},{4,6},{5,7},{6,4},{7,5},{8,10},{9,11},{10,... | collective-permute-start | bytes 2359304 | tf_op jit(solution)/shard_map/ppermute | solution.py:594
  24.9 34.4 %copy-start.1 = (bf16[1536,256]{1,0:T(8,128)(2,1)}, bf16[1536,256]{1,0:T(8,128)(2,1)S(1)}, u32[]{:S(2)}) copy-start(bf16[1536,256]{1,0:T(8,128)(2,1)S(1)} %collective-permute-done.refs_4_.refs_5_) | copy-start | bytes 2359300
  24.9 34.3 %collective-permute-start.4 = (bf16[1536,256]{1,0:T(8,128)(2,1)S(1)}, bf16[1536,256]{1,0:T(8,128)(2,1)S(1)}, u32[]{:S(2)}, u32[]{:S(2)}) collective-permute-start(bf16[1536,256]{1,0:T(8,128)(2,1)S(1)} %collective-permute-done.refs_4_.refs_5_), channel_id=1, source_target_pairs={{0,2},{1,3},{2,0},{3,1},{4,6},{5,7},{6,4},{7,5},{8,10},{9,11},{10,... | collective-permute-start | bytes 2359304 | tf_op jit(solution)/shard_map/ppermute | solution.py:594
  27.0 32.3 %copy-start.2 = (bf16[1536,256]{1,0:T(8,128)(2,1)}, bf16[1536,256]{1,0:T(8,128)(2,1)S(1)}, u32[]{:S(2)}) copy-start(bf16[1536,256]{1,0:T(8,128)(2,1)S(1)} %collective-permute-done.1.refs_5_.refs_6_) | copy-start | bytes 2359300
  27.0 32.2 %collective-permute-start.5 = (bf16[1536,256]{1,0:T(8,128)(2,1)S(1)}, bf16[1536,256]{1,0:T(8,128)(2,1)S(1)}, u32[]{:S(2)}, u32[]{:S(2)}) collective-permute-start(bf16[1536,256]{1,0:T(8,128)(2,1)S(1)} %collective-permute-done.1.refs_5_.refs_6_), channel_id=1, source_target_pairs={{0,1},{1,0},{2,3},{3,2},{4,5},{5,4},{6,7},{7,6},{8,9},{9,8},{10,11... | collective-permute-start | bytes 2359304 | tf_op jit(solution)/shard_map/ppermute | solution.py:594
  50.8 13.1 %copy-start.3 = (bf16[1536,256]{1,0:T(8,128)(2,1)}, bf16[1536,256]{1,0:T(8,128)(2,1)S(1)}, u32[]{:S(2)}) copy-start(bf16[1536,256]{1,0:T(8,128)(2,1)S(1)} %collective-permute-done.2.refs_6_.refs_7_) | copy-start | bytes 2359300
  50.8 13.1 %copy-start.4 = (bf16[1536,256]{1,0:T(8,128)(2,1)}, bf16[1536,256]{1,0:T(8,128)(2,1)S(1)}, u32[]{:S(2)}) copy-start(bf16[1536,256]{1,0:T(8,128)(2,1)S(1)} %collective-permute-done.3.refs_7_.refs_8_) | copy-start | bytes 2359300
  59.3 4.7 %copy-start.5 = (bf16[1536,256]{1,0:T(8,128)(2,1)}, bf16[1536,256]{1,0:T(8,128)(2,1)S(1)}, u32[]{:S(2)}) copy-start(bf16[1536,256]{1,0:T(8,128)(2,1)S(1)} %collective-permute-done.4.refs_8_.refs_9_) | copy-start | bytes 2359300
  59.3 4.7 %copy-start.6 = (bf16[1536,256]{1,0:T(8,128)(2,1)}, bf16[1536,256]{1,0:T(8,128)(2,1)S(1)}, u32[]{:S(2)}) copy-start(bf16[1536,256]{1,0:T(8,128)(2,1)S(1)} %collective-permute-done.5.refs_9_.refs_10_) | copy-start | bytes 2359300
  64.0 34.9 %collective-permute-start.6 = (s16[1568,256]{1,0:T(8,128)(2,1)}, s16[1568,256]{1,0:T(8,128)(2,1)S(1)}, u32[]{:S(2)}, u32[]{:S(2)}) collective-permute-start(s16[1568,256]{1,0:T(8,128)(2,1)} %get-tuple-element.17), channel_id=1, source_target_pairs={{0,1},{1,0},{2,3},{3,2},{4,5},{5,4},{6,7},{7,6},{8,9},{9,8},{10,11... | collective-permute-start | bytes 2408456 | tf_op jit(solution)/shard_map/ppermute | solution.py:594
  73.4 25.5 %collective-permute-start.7 = (s16[1568,256]{1,0:T(8,128)(2,1)}, s16[1568,256]{1,0:T(8,128)(2,1)S(1)}, u32[]{:S(2)}, u32[]{:S(2)}) collective-permute-start(s16[1568,256]{1,0:T(8,128)(2,1)} %get-tuple-element.18), channel_id=1, source_target_pairs={{0,2},{1,3},{2,0},{3,1},{4,6},{5,7},{6,4},{7,5},{8,10},{9,11},{10,... | collective-permute-start | bytes 2408456 | tf_op jit(solution)/shard_map/ppermute | solution.py:594
  73.4 1.9 %copy-start.7 = (bf16[6144,256]{1,0:T(8,128)(2,1)S(1)}, bf16[6144,256]{1,0:T(8,128)(2,1)}, u32[]{:S(2)}) copy-start(bf16[6144,256]{1,0:T(8,128)(2,1)} %get-tuple-element.21.refs_2_) | copy-start | bytes 9437188
  81.9 11.1 %collective-permute-start.10 = (f32[64,256]{1,0:T(8,128)S(1)}, f32[64,256]{1,0:T(8,128)S(1)}, u32[]{:S(2)}, u32[]{:S(2)}) collective-permute-start(f32[64,256]{1,0:T(8,128)S(1)} %get-tuple-element.24), channel_id=1, source_target_pairs={{0,4},{4,8},{8,12},{12,0},{1,5},{5,9},{9,13},{13,1},{2,6},{6,10},{... | collective-permute-start | bytes 196616 | tf_op jit(solution)/shard_map/ppermute | solution.py:563
  87.4 7.9 %collective-permute-start.11 = (f32[64,256]{1,0:T(8,128)S(1)}, f32[64,256]{1,0:T(8,128)S(1)}, u32[]{:S(2)}, u32[]{:S(2)}) collective-permute-start(f32[64,256]{1,0:T(8,128)S(1)} %get-tuple-element.26), channel_id=1, source_target_pairs={{0,8},{4,12},{8,0},{12,4},{1,9},{5,13},{9,1},{13,5},{2,10},{6,14},... | collective-permute-start | bytes 196616 | tf_op jit(solution)/shard_map/ppermute | solution.py:563
  90.7 4.6 %collective-permute-start.12 = (f32[64,256]{1,0:T(8,128)S(1)}, f32[64,256]{1,0:T(8,128)S(1)}, u32[]{:S(2)}, u32[]{:S(2)}) collective-permute-start(f32[64,256]{1,0:T(8,128)S(1)} %get-tuple-element.25), channel_id=1, source_target_pairs={{0,12},{4,0},{8,4},{12,8},{1,13},{5,1},{9,5},{13,9},{2,14},{6,2},{... | collective-permute-start | bytes 196616 | tf_op jit(solution)/shard_map/ppermute | solution.py:563
  95.3 6.0 %collective-permute-start.13 = (f32[64,256]{1,0:T(8,128)S(1)}, f32[64,256]{1,0:T(8,128)S(1)}, u32[]{:S(2)}, u32[]{:S(2)}) collective-permute-start(f32[64,256]{1,0:T(8,128)S(1)} %add_add_fusion.refs_0_), channel_id=1, source_target_pairs={{0,1},{1,0},{2,3},{3,2},{4,5},{5,4},{6,7},{7,6},{8,9},{9,8},{10,11... | collective-permute-start | bytes 196616 | tf_op jit(solution)/shard_map/ppermute | solution.py:594
  95.4 6.0 %collective-permute-start.14 = (f32[64,256]{1,0:T(8,128)S(1)}, f32[64,256]{1,0:T(8,128)S(1)}, u32[]{:S(2)}, u32[]{:S(2)}) collective-permute-start(f32[64,256]{1,0:T(8,128)S(1)} %add_add_fusion.refs_0_), channel_id=1, source_target_pairs={{0,2},{1,3},{2,0},{3,1},{4,6},{5,7},{6,4},{7,5},{8,10},{9,11},{10,... | collective-permute-start | bytes 196616 | tf_op jit(solution)/shard_map/ppermute | solution.py:594
  96.9 5.2 %collective-permute-start.15 = (f32[64,256]{1,0:T(8,128)S(1)}, f32[64,256]{1,0:T(8,128)S(1)}, u32[]{:S(2)}, u32[]{:S(2)}) collective-permute-start(f32[64,256]{1,0:T(8,128)S(1)} %add_add_fusion.refs_0_), channel_id=1, source_target_pairs={{0,3},{1,2},{2,1},{3,0},{4,7},{5,6},{6,5},{7,4},{8,11},{9,10},{10,... | collective-permute-start | bytes 196616 | tf_op jit(solution)/shard_map/ppermute | solution.py:594
  98.9 11.5 %copy-start.9 = (f32[1,256,256]{2,1,0:T(8,128)S(1)}, f32[1,256,256]{2,1,0:T(8,128)}, u32[]{:S(2)}) copy-start(f32[1,256,256]{2,1,0:T(8,128)} %param.7) | copy-start | bytes 786436
  102.1 6.5 %collective-permute-start.16 = (f32[64,256]{1,0:T(8,128)S(1)}, f32[64,256]{1,0:T(8,128)S(1)}, u32[]{:S(2)}, u32[]{:S(2)}) collective-permute-start(f32[64,256]{1,0:T(8,128)S(1)} %added.1), channel_id=1, source_target_pairs={{0,4},{4,8},{8,12},{12,0},{1,5},{5,9},{9,13},{13,1},{2,6},{6,10},{... | collective-permute-start | bytes 196616 | tf_op jit(solution)/shard_map/ppermute | solution.py:563
  103.9 6.1 %collective-permute-start.17 = (f32[64,256]{1,0:T(8,128)S(1)}, f32[64,256]{1,0:T(8,128)S(1)}, u32[]{:S(2)}, u32[]{:S(2)}) collective-permute-start(f32[64,256]{1,0:T(8,128)S(1)} %added.1), channel_id=1, source_target_pairs={{0,8},{4,12},{8,0},{12,4},{1,9},{5,13},{9,1},{13,5},{2,10},{6,14},... | collective-permute-start | bytes 196616 | tf_op jit(solution)/shard_map/ppermute | solution.py:563
  105.4 5.0 %collective-permute-start.18 = (f32[64,256]{1,0:T(8,128)S(1)}, f32[64,256]{1,0:T(8,128)S(1)}, u32[]{:S(2)}, u32[]{:S(2)}) collective-permute-start(f32[64,256]{1,0:T(8,128)S(1)} %added.1), channel_id=1, source_target_pairs={{0,12},{4,0},{8,4},{12,8},{1,13},{5,1},{9,5},{13,9},{2,14},{6,2},{... | collective-permute-start | bytes 196616 | tf_op jit(solution)/shard_map/ppermute | solution.py:563
  106.3 8.9 %collective-permute-start.8 = (s16[784,256]{1,0:T(8,128)(2,1)S(1)}, s16[784,256]{1,0:T(8,128)(2,1)S(1)}, u32[]{:S(2)}, u32[]{:S(2)}) collective-permute-start(s16[784,256]{1,0:T(8,128)(2,1)S(1)} %get-tuple-element.19.refs_4_), channel_id=1, source_target_pairs={{0,2},{1,3},{2,0},{3,1},{4,6},{5,7},{6,4},{7,5},{8,10},{9,11},{10,... | collective-permute-start | bytes 1204232 | tf_op jit(solution)/shard_map/ppermute | solution.py:594
  107.1 8.9 %collective-permute-start.9 = (s16[784,256]{1,0:T(8,128)(2,1)S(1)}, s16[784,256]{1,0:T(8,128)(2,1)S(1)}, u32[]{:S(2)}, u32[]{:S(2)}) collective-permute-start(s16[784,256]{1,0:T(8,128)(2,1)S(1)} %get-tuple-element.20), channel_id=1, source_target_pairs={{0,1},{1,0},{2,3},{3,2},{4,5},{5,4},{6,7},{7,6},{8,9},{9,8},{10,11... | collective-permute-start | bytes 1204232 | tf_op jit(solution)/shard_map/ppermute | solution.py:594

commit v2 on v1

v2 whole, which is shorter than its diff:
```python
import functools

import jax
import jax.numpy as jnp
from jax import lax
from jax.experimental import pallas as pl
from jax.experimental.pallas import tpu as pltpu
from jax.sharding import PartitionSpec as P
import math

LANES = 128
TILE = 256
WINDOW = TILE + LANES
STRIP = 2 * TILE
SLOTS = 3
GROUP = 64
STEPS = 256.0
TOP = 32766.0
ROUND = 12582912.0
LIMIT = 40 * 1024 * 1024
FIRST = 3
KERNELS = 4
GROUP_TILES = 4
SMALL = pl.CostEstimate(flops=1000, bytes_accessed=1000, transcendentals=0)
LAST = 3


class Layout:
    def __init__(self, rows, cols):
        self.strips = cols // STRIP
        self.col_tiles = cols // TILE
        self.row_tiles = rows // TILE
        self.counts = 0
        self.lists = KERNELS
        self.col_begins = self.lists + KERNELS * self.strips
        self.row_begins = self.col_begins + self.col_tiles
        self.row_phases = self.row_begins + self.row_tiles
        self.me = self.row_phases + self.row_tiles
        self.col_base = self.me + 1
        self.row_base = self.me + 2
        self.row = self.me + 3
        self.size = self.me + 4


def near_half(shard):
    return 1 - lax.rem(shard, 2)


def arrival(block, me):
    shard = lax.div(block, 2)
    near = lax.rem(block, 2) == near_half(shard)
    away = shard ^ me
    beside = jnp.where(near == (away == 1), 1, 3)
    return jnp.where(away == 0, 0, jnp.where(away == 3, 2, beside))


def plan_kernel(at, half, total_rows, before, place, plan):
    me = place[0]

    def phase(first, last):
        start = arrival(lax.div(first, half), me)
        end = arrival(lax.div(last - 1, half), me)
        return jnp.maximum(start, end)

    def begin(first):
        return jnp.minimum(lax.div(first, LANES) * LANES, total_rows - WINDOW)

    for i in range(KERNELS * at.strips):
        plan[at.lists + i] = 0
    counts = [jnp.int32(0)] * KERNELS
    per = STRIP // TILE
    for s in range(at.strips):
        first, last = before[s * per], before[(s + 1) * per]
        when = phase(first, last)
        some = last > first
        taken = jnp.bool_(False)
        for j in range(KERNELS):
            fits = some & (when <= j) & ~taken
            if j == 0:
                fits = fits & (counts[j] < FIRST)

            @pl.when(fits)
            def _():
                plan[at.lists + j * at.strips + counts[j]] = s

            counts[j] = counts[j] + jnp.where(fits, 1, 0)
            taken = taken | fits
    for j in range(KERNELS):
        plan[at.counts + j] = counts[j]
    for k in range(at.col_tiles):
        plan[at.col_begins + k] = begin(before[k])
    base = at.col_tiles + 1
    for k in range(at.row_tiles):
        first, last = before[base + k], before[base + k + 1]
        plan[at.row_begins + k] = begin(first)
        plan[at.row_phases + k] = jnp.where(last > first, phase(first, last), 0)
    for i in range(4):
        plan[at.me + i] = place[i]


def make_plan(at, half, total_rows, before, place):
    smem = pl.BlockSpec(memory_space=pltpu.SMEM)
    return pl.pallas_call(
        functools.partial(plan_kernel, at, half, total_rows),
        in_specs=[smem, smem],
        out_specs=smem,
        out_shape=jax.ShapeDtypeStruct((at.size,), jnp.int32),
        compiler_params=pltpu.CompilerParams(vmem_limit_bytes=LIMIT),
        cost_estimate=SMALL,
        name="plan",
    )(before, place)


def halves_kernel(which, own, first, second, sems):
    half = first.shape[0]
    copies = [
        pltpu.make_async_copy(own.at[pl.ds(pl.multiple_of(part * half, LANES), half)], out, sems.at[n])
        for n, (part, out) in enumerate(((which[0], first), (1 - which[0], second)))
    ]
    for copy in copies:
        copy.start()
    for copy in copies:
        copy.wait()


def halves(which, own):
    piece = pltpu.VMEM((own.shape[0] // 2, own.shape[1]), own.dtype)
    vmem = pl.BlockSpec(memory_space=pltpu.VMEM)
    return pl.pallas_call(
        halves_kernel,
        in_specs=[pl.BlockSpec(memory_space=pltpu.SMEM), pl.BlockSpec(memory_space=pltpu.HBM)],
        out_specs=[vmem, vmem],
        out_shape=[piece, piece],
        scratch_shapes=[pltpu.SemaphoreType.DMA((2,))],
        compiler_params=pltpu.CompilerParams(vmem_limit_bytes=LIMIT),
        cost_estimate=SMALL,
        name="halves",
    )(which, own)


def window_hits(map_ref, begin, target):
    first = lax.div(begin, LANES)
    row = jnp.concatenate([map_ref[first + j] for j in range(WINDOW // LANES)], axis=1)
    wanted = lax.broadcasted_iota(jnp.int32, (TILE, WINDOW), 0) + target
    return wanted == row


def spread_tile(panel_ref, map_ref, begin, target):
    table = jnp.where(window_hits(map_ref, begin, target), 1.0, 0.0).astype(jnp.bfloat16)
    rows = panel_ref[pl.ds(pl.multiple_of(begin, LANES), WINDOW), :]
    return jnp.dot(table, rows, preferred_element_type=jnp.float32).astype(jnp.bfloat16)


def strip_tile(at, s, plan, map_ref, panel, strip):
    per = STRIP // TILE
    for t in range(per):
        k = s * per + t
        strip[t * TILE:(t + 1) * TILE, :] = spread_tile(
            panel, map_ref, plan[at.col_begins + k], plan[at.col_base] + k * TILE
        )


def half_block(shard, near):
    return shard * 2 + (near_half(shard) if near else 1 - near_half(shard))


def piece_blocks(me):
    return [
        me,
        half_block(me ^ 1, True), half_block(me ^ 2, False),
        half_block(me ^ 3, True), half_block(me ^ 3, False),
        half_block(me ^ 1, False), half_block(me ^ 2, True),
    ]


def panel_copies(me, pieces, panel, sems):
    copies = []
    for n, (piece, block) in enumerate(zip(pieces, piece_blocks(me))):
        size = piece.shape[0]
        copies.append(
            pltpu.make_async_copy(piece, panel.at[pl.ds(pl.multiple_of(block * size, LANES), size)], sems.at[n])
        )
    return copies


def clear_panel(step, me, half, panel):
    for block in range(panel.shape[0] // half):
        @pl.when(arrival(jnp.int32(block), me) > step)
        def _():
            panel[block * half:(block + 1) * half, :] = jnp.zeros((half, panel.shape[1]), panel.dtype)


def row_tile(at, k, plan, map_ref, panel):
    return spread_tile(panel, map_ref, plan[at.row_begins + k], plan[at.row_base] + k * TILE)


def build_rows(at, first, last, plan, map_ref, panel, tiles, spread, sems):
    def written(k):
        return pltpu.make_async_copy(
            tiles.at[k], spread.at[pl.ds(pl.multiple_of(k * TILE, TILE), TILE)], sems.at[0]
        )

    def chosen(k):
        phase = plan[at.row_phases + k]
        return (phase >= first) & (phase <= last)

    @pl.loop(0, at.row_tiles)
    def _(k):
        @pl.when(chosen(k))
        def _():
            tiles[k] = row_tile(at, k, plan, map_ref, panel)
            written(k).start()

    @pl.loop(0, at.row_tiles)
    def _(k):
        pl.when(chosen(k))(lambda: written(k).wait())


def fetched(at, j, plan, front, fronts, sems, i):
    s = plan[at.lists + j * at.strips + i]
    slot = lax.rem(i, SLOTS)
    return pltpu.make_async_copy(
        front.at[:, pl.ds(pl.multiple_of(s * STRIP, STRIP), STRIP)], fronts.at[slot], sems.at[slot]
    )


def strips_begin(at, j, plan, front, fronts, sems, i):
    @pl.when(i < plan[at.counts + j])
    def _():
        fetched(at, j, plan, front, fronts, sems, jnp.int32(i)).start()


def begin(at, j, plan, front, fronts, sems, pieces, panel, own_sems, arriving):
    copies = panel_copies(plan[at.me], pieces, panel, own_sems)
    for copy in copies:
        copy.start()
    strips_begin(at, j, plan, front, fronts, sems, 0)
    for copy in arriving:
        copy.start()
    for i in range(1, SLOTS - 1):
        strips_begin(at, j, plan, front, fronts, sems, i)
    if j < LAST:
        clear_panel(j, plan[at.me], pieces[0].shape[0] // 2, panel)
    for copy in copies:
        copy.wait()


def strips_loop(at, j, plan, front, fronts, sems, map_ref, panel, strips, total):
    count = plan[at.counts + j]
    listed = at.lists + j * at.strips

    @pl.when(count > 0)
    def _():
        strip_tile(at, plan[listed], plan, map_ref, panel, strips.at[0])

    @pl.loop(0, count)
    def _(i):
        @pl.when(i + SLOTS - 1 < count)
        def _():
            fetched(at, j, plan, front, fronts, sems, i + SLOTS - 1).start()

        now = lax.rem(i, 2)
        following = plan[listed + jnp.minimum(i + 1, count - 1)]
        fetched(at, j, plan, front, fronts, sems, i).wait()
        total[...] += jnp.dot(fronts[lax.rem(i, SLOTS)], strips[now], preferred_element_type=jnp.float32)
        strip_tile(at, following, plan, map_ref, panel, strips.at[1 - now])


def first_kernel(at, plan, front, map_ref, own, out, total, fronts, panel, strips, sems, own_sems):
    begin(at, 0, plan, front, fronts, sems, [own], panel, own_sems, [])
    total[...] = jnp.zeros_like(total)
    strips_loop(at, 0, plan, front, fronts, sems, map_ref, panel, strips, total)
    leaving = pltpu.make_async_copy(total, out, own_sems.at[0])
    leaving.start()
    leaving.wait()


def next_kernel(at, j, n_pieces, *refs):
    plan, front, map_ref = refs[:3]
    pieces = refs[3:3 + n_pieces]
    start = refs[3 + n_pieces]
    total, spread, tiles, fronts, panel, strips, sems, own_sems = refs[-8:]
    first = 0 if j == 1 else j
    wanted = plan[at.counts + j] > 0
    for k in range(at.row_tiles):
        wanted = wanted | ((plan[at.row_phases + k] >= first) & (plan[at.row_phases + k] <= j))
    arriving = [pltpu.make_async_copy(start, total, own_sems.at[n_pieces])] if j == 1 else []

    @pl.when(wanted)
    def _():
        begin(at, j, plan, front, fronts, sems, pieces, panel, own_sems, arriving)

    if j == 1:
        @pl.when(~wanted)
        def _():
            arriving[0].start()

        arriving[0].wait()

    @pl.when(wanted)
    def _():
        strips_loop(at, j, plan, front, fronts, sems, map_ref, panel, strips, total)
        build_rows(at, first, j, plan, map_ref, panel, tiles, spread, own_sems)


def strips_call(kernel, at, plan, front, map3, others, out_specs, out_shape, scratch, expected, name, carried=()):
    rows = front.shape[0]
    width = others[0].shape[1]
    vmem = pl.BlockSpec(memory_space=pltpu.VMEM)
    smem = pl.BlockSpec(memory_space=pltpu.SMEM)
    hbm = pl.BlockSpec(memory_space=pltpu.HBM)
    return pl.pallas_call(
        functools.partial(kernel, at),
        in_specs=[smem, hbm, vmem] + [hbm] * len(others) + [vmem, hbm][:len(carried)],
        out_specs=out_specs,
        scratch_shapes=scratch + [
            pltpu.VMEM((SLOTS, rows, STRIP), jnp.bfloat16),
            pltpu.VMEM((map3.shape[0] * LANES, width), jnp.bfloat16),
            pltpu.VMEM((2, STRIP, width), jnp.bfloat16),
            pltpu.SemaphoreType.DMA((SLOTS,)),
            pltpu.SemaphoreType.DMA((len(others) + 2,)),
        ],
        out_shape=out_shape,
        input_output_aliases={3 + len(others) + n: n for n in range(len(carried))},
        compiler_params=pltpu.CompilerParams(vmem_limit_bytes=LIMIT),
        cost_estimate=pl.CostEstimate(
            flops=8 * rows * STRIP * width * expected, bytes_accessed=8 * rows * STRIP * expected, transcendentals=0
        ),
        name=name,
    )(plan, front, map3, *others, *carried)


def first_strips(at, plan, front, map3, own):
    shape = front.shape[0], own.shape[1]
    return strips_call(
        first_kernel, at, plan, front, map3, [own], [pl.BlockSpec(memory_space=pltpu.HBM)],
        [pltpu.HBM(shape, jnp.float32)], [pltpu.VMEM(shape, jnp.float32)], FIRST, "strips_0",
    )[0]


def next_strips(at, j, plan, front, map3, pieces, start, spread=None):
    rows, width = start.shape
    return strips_call(
        lambda at, *refs: next_kernel(at, j, len(pieces), *refs), at, plan, front, map3,
        pieces + [start] * (j == 1), [pl.BlockSpec(memory_space=pltpu.VMEM), pl.BlockSpec(memory_space=pltpu.HBM)],
        [pltpu.VMEM(start.shape, start.dtype), pltpu.HBM((rows, width), jnp.bfloat16)],
        [pltpu.VMEM((at.row_tiles, TILE, width), jnp.bfloat16)], at.strips, f"strips_{j}", [start, spread][:2 * (j == 2)],
    )


def quantized(values, out_ref):
    rows, width = values.shape[0], values.shape[1]
    codes = []
    for g in range(rows // GROUP):
        part = values[g * GROUP:(g + 1) * GROUP, :]
        most = jnp.max(jnp.abs(part), axis=0, keepdims=True)
        code = jnp.clip(jnp.ceil(jnp.log2(jnp.maximum(most, 1e-30)) * STEPS) + 1.0, -32000.0, 32000.0)
        inverse = TOP / jnp.exp2(code * (1.0 / STEPS))
        whole = ((part * inverse + ROUND) - ROUND).astype(jnp.int32)
        out_ref[g * GROUP:(g + 1) * GROUP, :] = whole.astype(jnp.int16)
        codes.append(code)
    codes.append(jnp.zeros((out_ref.shape[0] - rows - len(codes), width), jnp.float32))
    tail = jnp.concatenate(codes, axis=0).astype(jnp.int32)
    out_ref[rows:, :] = tail.astype(jnp.int16)


def coded_rows(rows):
    return rows + (rows // GROUP + 15) // 16 * 16


def decoded(ref, rows):
    codes = ref[rows:, :].astype(jnp.int32).astype(jnp.float32)
    scales = jnp.exp2(codes * (1.0 / STEPS)) * (1.0 / TOP)
    parts = []
    for g in range(rows // GROUP):
        part = ref[g * GROUP:(g + 1) * GROUP, :].astype(jnp.int32).astype(jnp.float32)
        parts.append(part * scales[g:g + 1, :])
    return jnp.concatenate(parts, axis=0)


def part_of(total, which, part):
    half = total.shape[0] // 8
    return total[pl.ds(pl.multiple_of((which * 2 + part) * half, half), half), :]


def last_strips_kernel(at, n_pieces, *refs):
    plan, front, map_ref = refs[:3]
    pieces = refs[3:3 + n_pieces]
    total, x_out, y_out, written, fronts, panel, strips, sems, own_sems = refs[4 + n_pieces:]
    me = plan[at.me]
    j = KERNELS - 1

    @pl.when(plan[at.counts + j] > 0)
    def _():
        begin(at, j, plan, front, fronts, sems, pieces, panel, own_sems, [])
        strips_loop(at, j, plan, front, fronts, sems, map_ref, panel, strips, total)

    copy = pltpu.make_async_copy(total, written, own_sems.at[0])
    copy.start()
    coded = x_out.shape[0] // 2
    quantized(part_of(total, me ^ 3, 0), x_out.at[:coded])
    quantized(part_of(total, me ^ 1, 0), x_out.at[coded:])
    quantized(part_of(total, me ^ 3, 1), y_out.at[:coded])
    quantized(part_of(total, me ^ 2, 1), y_out.at[coded:])
    copy.wait()


def last_strips(at, plan, front, map3, pieces, total):
    rows, width = total.shape
    coded = coded_rows(rows // 8)
    vmem = pl.BlockSpec(memory_space=pltpu.VMEM)
    smem = pl.BlockSpec(memory_space=pltpu.SMEM)
    hbm = pl.BlockSpec(memory_space=pltpu.HBM)
    return pl.pallas_call(
        functools.partial(last_strips_kernel, at, len(pieces)),
        in_specs=[smem, hbm, vmem] + [hbm] * len(pieces) + [vmem],
        out_specs=[vmem] * 3 + [hbm],
        scratch_shapes=[
            pltpu.VMEM((SLOTS, rows, STRIP), jnp.bfloat16),
            pltpu.VMEM((map3.shape[0] * LANES, width), jnp.bfloat16),
            pltpu.VMEM((2, STRIP, width), jnp.bfloat16),
            pltpu.SemaphoreType.DMA((SLOTS,)),
            pltpu.SemaphoreType.DMA((len(pieces),)),
        ],
        out_shape=[
            pltpu.VMEM(total.shape, total.dtype),
        ] + [jax.ShapeDtypeStruct((2 * coded, width), jnp.int16)] * 2 + [pltpu.HBM(total.shape, total.dtype)],
        input_output_aliases={3 + len(pieces): 0},
        compiler_params=pltpu.CompilerParams(vmem_limit_bytes=LIMIT),
        cost_estimate=SMALL,
        name="last_strips",
    )(plan, front, map3, *pieces, total)[1:]


def diag_kernel(at, n_pieces, *refs):
    plan, total, early, map_ref = refs[:4]
    pieces = refs[4:4 + n_pieces]
    outs = refs[4 + n_pieces:-6]
    sums, values, lefts, panel, block_sems, sems = refs[-6:]
    groups, rows = values.shape[:2]
    row_tiles = rows // TILE

    def late(k):
        return plan[at.row_phases + k] == LAST

    def some_late(first, n):
        found = late(first)
        for k in range(1, n):
            found = found | late(first + k)
        return found

    def blocks(group):
        place = pl.ds(pl.multiple_of(group * rows, rows), rows)
        return [
            pltpu.make_async_copy(total.at[place], values.at[group], block_sems.at[0, group]),
            pltpu.make_async_copy(early.at[place], lefts.at[group], block_sems.at[1, group]),
        ]

    def add(group):
        high = values[group].astype(jnp.bfloat16)
        low = (values[group] - high.astype(jnp.float32)).astype(jnp.bfloat16)
        sums[...] += lax.dot_general(
            lefts[group], jnp.concatenate([high, low], axis=1), (((0,), (0,)), ((), ())),
            preferred_element_type=jnp.float32,
        )

    for group in range(groups):
        for copy in blocks(group):
            copy.start()
    any_late = some_late(0, at.row_tiles)
    copies = panel_copies(plan[at.me], pieces, panel, sems)

    @pl.when(any_late)
    def _():
        for copy in copies:
            copy.start()

    sums[...] = jnp.zeros_like(sums)

    @pl.loop(0, groups)
    def _(group):
        for copy in blocks(group):
            copy.wait()

        @pl.when(~some_late(group * row_tiles, row_tiles))
        def _():
            add(group)

    @pl.when(any_late)
    def _():
        for copy in copies:
            copy.wait()

        @pl.loop(0, groups)
        def _(group):
            @pl.when(some_late(group * row_tiles, row_tiles))
            def _():
                for t in range(row_tiles):
                    k = group * row_tiles + t

                    @pl.when(late(k))
                    def _():
                        lefts[group, t * TILE:(t + 1) * TILE, :] = row_tile(at, k, plan, map_ref, panel)

                add(group)

    share, width = outs[0].shape
    for by, out in enumerate(outs):
        place = pl.ds(pl.multiple_of(lax.rem(plan[at.row] + by, len(outs)) * share, share), share)
        out[...] = sums[place, :width] + sums[place, width:]


def diag_product(at, plan, map3, pieces, early, total, shares):
    rows, width = total.shape
    chunk = GROUP_TILES * TILE
    vmem = pl.BlockSpec(memory_space=pltpu.VMEM)
    hbm = pl.BlockSpec(memory_space=pltpu.HBM)
    return pl.pallas_call(
        functools.partial(diag_kernel, at, len(pieces)),
        in_specs=[pl.BlockSpec(memory_space=pltpu.SMEM), hbm, hbm, vmem] + [hbm] * len(pieces),
        out_specs=[vmem] * shares,
        out_shape=[jax.ShapeDtypeStruct((width // shares, width), jnp.float32)] * shares,
        scratch_shapes=[
            pltpu.VMEM((width, 2 * width), jnp.float32),
            pltpu.VMEM((rows // chunk, chunk, width), jnp.float32),
            pltpu.VMEM((rows // chunk, chunk, width), jnp.bfloat16),
            pltpu.VMEM((map3.shape[0] * LANES, width), jnp.bfloat16),
            pltpu.SemaphoreType.DMA((2, rows // chunk)),
            pltpu.SemaphoreType.DMA((len(pieces),)),
        ],
        compiler_params=pltpu.CompilerParams(vmem_limit_bytes=LIMIT),
        cost_estimate=SMALL,
        name="diag_product",
    )(plan, total, early, map3, *pieces)


def second_kernel(plan, low_ref, high_ref, x_in, y_in, *refs):
    terms, (low_out, high_out, sum_out) = refs[:-3], refs[-3:]
    rows = low_ref.shape[0]
    quantized(low_ref[...] + decoded(x_in, rows), low_out)
    quantized(high_ref[...] + decoded(y_in, rows), high_out)
    sum_out[...] = sum((term[...] for term in terms[1:]), terms[0][...])


def second_hop(at, plan, total, x_in, y_in, terms):
    half, width = total.shape[0] // 8, total.shape[1]
    coded = x_in.shape[0] // 2
    payload = pl.BlockSpec((coded, width), lambda i, plan: (0, 0))
    term = pl.BlockSpec(terms[0].shape, lambda i, plan: (0, 0))
    return pl.pallas_call(
        second_kernel,
        grid_spec=pltpu.PrefetchScalarGridSpec(
            num_scalar_prefetch=1,
            grid=(1,),
            in_specs=[
                pl.BlockSpec((half, width), lambda i, plan: ((plan[at.me] ^ 2) * 2, 0)),
                pl.BlockSpec((half, width), lambda i, plan: ((plan[at.me] ^ 1) * 2 + 1, 0)),
                payload,
                payload,
            ] + [term] * len(terms),
            out_specs=[payload, payload, term],
        ),
        out_shape=[jax.ShapeDtypeStruct((coded, width), jnp.int16)] * 2
        + [jax.ShapeDtypeStruct(terms[0].shape, jnp.float32)],
        compiler_params=pltpu.CompilerParams(vmem_limit_bytes=LIMIT),
        cost_estimate=SMALL,
        name="second_hop",
    )(plan, total, total, x_in, y_in, *terms)


def gate_kernel(n, *refs):
    sems = refs[-1]
    copies = [
        pltpu.make_async_copy(source, out, sems.at[i]) for i, (source, out) in enumerate(zip(refs[:n], refs[n:2 * n]))
    ]
    for copy in copies:
        copy.start()
    for copy in copies:
        copy.wait()


def gated(values):
    return pl.pallas_call(
        functools.partial(gate_kernel, len(values)),
        in_specs=[pl.BlockSpec(memory_space=pl.ANY)] * len(values),
        out_specs=[pl.BlockSpec(memory_space=pltpu.VMEM)] * len(values),
        out_shape=[pltpu.VMEM(value.shape, value.dtype) for value in values],
        scratch_shapes=[pltpu.SemaphoreType.DMA((len(values),))],
        compiler_params=pltpu.CompilerParams(vmem_limit_bytes=LIMIT),
        cost_estimate=SMALL,
        name="gated",
    )(*values)


def last_kernel(at, plan, low_ref, high_ref, x_in, y_in, low_in, high_in, map_ref, out_ref):
    me = plan[at.me]
    rows = low_ref.shape[0]
    tiles = rows // TILE
    sums = [
        low_ref[...] + decoded(x_in, rows) + decoded(low_in, rows),
        high_ref[...] + decoded(y_in, rows) + decoded(high_in, rows),
    ]
    for part, value in enumerate(sums):
        for j in range(tiles):
            n = part * tiles + j
            k = me * 2 * tiles + n
            hits = window_hits(map_ref, plan[at.row_begins + k], plan[at.row_base] + k * TILE)
            marked = jnp.max(jnp.where(hits, 1.0, 0.0), axis=1, keepdims=True)
            tile = value[j * TILE:(j + 1) * TILE, :]
            out_ref[n * TILE:(n + 1) * TILE, :] = jnp.where(marked > 0.5, -tile, 0.0)


def last_sum(at, plan, total, x_in, y_in, low_in, high_in, map3):
    half, width = total.shape[0] // 8, total.shape[1]
    first = pl.BlockSpec(low_in.shape, lambda i, plan: (0, 0))
    second = pl.BlockSpec(low_in.shape, lambda i, plan: (1, 0))
    return pl.pallas_call(
        functools.partial(last_kernel, at),
        grid_spec=pltpu.PrefetchScalarGridSpec(
            num_scalar_prefetch=1,
            grid=(1,),
            in_specs=[
                pl.BlockSpec((half, width), lambda i, plan: (plan[at.me] * 2, 0)),
                pl.BlockSpec((half, width), lambda i, plan: (plan[at.me] * 2 + 1, 0)),
                second, second, first, first,
                pl.BlockSpec(map3.shape, lambda i, plan: (0, 0, 0)),
            ],
            out_specs=pl.BlockSpec((2 * half, width), lambda i, plan: (0, 0)),
        ),
        out_shape=pltpu.HBM((2 * half, width), jnp.float32),
        compiler_params=pltpu.CompilerParams(vmem_limit_bytes=LIMIT),
        cost_estimate=SMALL,
        name="last_sum",
    )(plan, total, total, x_in, y_in, low_in, high_in, map3)


def together_kernel(at, plan, start, *refs):
    shares, out = refs[:-1], refs[-1]
    for by, share in enumerate(shares):
        size = share.shape[0]
        place = pl.ds(pl.multiple_of(lax.rem(plan[at.row] - by + len(shares), len(shares)) * size, size), size)
        out[place, :] = start[place, :] + share[...]


def together(at, plan, start, shares):
    vmem = pl.BlockSpec(memory_space=pltpu.VMEM)
    return pl.pallas_call(
        functools.partial(together_kernel, at),
        in_specs=[pl.BlockSpec(memory_space=pltpu.SMEM), vmem] + [vmem] * len(shares),
        out_specs=vmem,
        out_shape=jax.ShapeDtypeStruct(start.shape, start.dtype),
        compiler_params=pltpu.CompilerParams(vmem_limit_bytes=LIMIT),
        cost_estimate=SMALL,
        name="together",
    )(plan, start, *shares)


def four_columns(front, panel, row_map, diag_inverse):
    me = lax.axis_index("col")
    rows, cols = front.shape
    own = panel[0]
    half = own.shape[0] // 2
    places = row_map[0]
    map3 = places.reshape(-1, 1, LANES)
    total_rows = places.shape[0]
    at = Layout(rows, cols)

    def partner(value, bit):
        return lax.ppermute(value, "col", [(i, i ^ bit) for i in range(4)])

    def shifted(value, by):
        n = lax.axis_size("row")
        return lax.ppermute(value, "row", [(i, (i + by) % n) for i in range(n)])

    def in_hbm(value):
        return pltpu.with_memory_space_constraint(value, pltpu.HBM)

    own = in_hbm(own)
    near, far = halves(near_half(me).reshape(1), own)
    x_near = partner(near, 1)
    y_far = partner(far, 2)

    col_base = me * cols
    row_base = lax.axis_index("row") * rows
    marks = jnp.concatenate([
        col_base + TILE * jnp.arange(cols // TILE + 1, dtype=jnp.int32),
        row_base + TILE * jnp.arange(rows // TILE + 1, dtype=jnp.int32),
    ])
    before = jnp.sum(places[None, :] < marks[:, None], axis=1, dtype=jnp.int32)
    place = jnp.stack([me, col_base, row_base, lax.axis_index("row")]).astype(jnp.int32)
    plan = make_plan(at, half, total_rows, before, place)

    pieces = [own]
    start = first_strips(at, plan, front, map3, own)
    far, near, x_on, y_on = gated([far, near, x_near, y_far])
    d_near = partner(x_on, 2)
    d_far = partner(y_on, 1)
    x_far = partner(far, 1)
    y_near = partner(near, 2)
    pieces += [x_near, y_far]
    total, early = next_strips(at, 1, plan, front, map3, pieces, in_hbm(start))
    pieces += [d_near, d_far]
    total, early = next_strips(at, 2, plan, front, map3, pieces, total, early)
    pieces += [x_far, y_near]
    to_x, to_y, total = last_strips(at, plan, front, map3, pieces, total)

    total = in_hbm(total)
    from_x, from_y = partner(to_x, 1), partner(to_y, 2)
    n = lax.axis_size("row")
    terms = diag_product(at, plan, map3, [in_hbm(piece) for piece in pieces], in_hbm(early), total, n)
    mine = sum((shifted(terms[by], by) for by in range(1, n)), terms[0])
    terms = [mine] + [partner(mine, bit) for bit in (1, 2, 3)]
    low, high, mine = second_hop(at, plan, total, from_x, from_y, terms)
    low = partner(low, 2)
    high = partner(high, 1)
    offdiag = last_sum(at, plan, total, from_x, from_y, low, high, map3)
    diag = together(at, plan, diag_inverse[0], [mine] + [shifted(mine, by) for by in range(1, n)])
    return offdiag[None], diag[None]


def spread_range(padded_rows, padded_places, places, lower, count):
    blk = math.gcd(count, 128)
    nblk = count // blk
    starts = lower + jnp.arange(nblk, dtype=jnp.int32) * blk
    first = jnp.searchsorted(places, starts)

    def window(begin):
        rows = lax.dynamic_slice_in_dim(padded_rows, begin, blk, 0)
        marks = lax.dynamic_slice_in_dim(padded_places, begin, blk, 0)
        return (rows, marks)

    rows, marks = jax.vmap(window)(first)
    target = starts[:, None] + jnp.arange(blk, dtype=jnp.int32)[None, :]
    onehot = marks[:, None, :] == target[:, :, None]
    table = onehot.astype(jnp.bfloat16)
    spread = jnp.einsum("njk,nkw->njw", table, rows, preferred_element_type=jnp.float32)
    hits = jnp.sum(onehot.astype(jnp.float32), axis=2)
    return (spread.astype(jnp.bfloat16).reshape(count, rows.shape[2]), hits.reshape(count))


def any_columns(front_inverse, panel, row_map, diag_inverse):
    row_index = lax.axis_index("row")
    col_index = lax.axis_index("col")
    ncol = lax.axis_size("col")
    front_rows, front_cols = front_inverse.shape
    share = front_rows // ncol
    width = panel.shape[2]
    col_lower = col_index * front_cols
    row_lower = row_index * front_rows
    share_lower = row_lower + col_index * share
    places_all = row_map[0]
    whole_panel = lax.all_gather(panel, "col", axis=1, tiled=True)[0]
    padded_rows = jnp.concatenate([whole_panel, jnp.zeros((128, width), jnp.bfloat16)], axis=0)
    total_front = front_rows * lax.axis_size("row")
    padded_places = jnp.concatenate([places_all, jnp.full((128,), total_front, jnp.int32)], axis=0)
    spread_cols, unused_hits = spread_range(
        padded_rows, padded_places, places_all, col_lower, front_cols
    )
    spread_rows, share_hits = spread_range(
        padded_rows, padded_places, places_all, share_lower, share
    )
    product = lax.psum_scatter(
        jnp.dot(front_inverse, spread_cols, preferred_element_type=jnp.float32),
        "col",
        scatter_dimension=0,
        tiled=True,
    )
    local_terms = jnp.dot(
        spread_rows.astype(jnp.float32).T, product, precision=lax.Precision.HIGHEST
    )
    diag_terms = lax.psum(local_terms, ("row", "col"))
    offdiag = jnp.where(share_hits[:, None] > 0.5, -product, jnp.zeros_like(product))
    diag = diag_inverse[0] + diag_terms
    return (offdiag[None], diag[None])


def solution(mesh):
    return jax.shard_map(
        four_columns if mesh.shape["col"] == 4 else any_columns,
        mesh=mesh,
        in_specs=(P("row", "col"), P("sib", "col", None), P("sib", None), P("sib", None, None)),
        out_specs=(P("sib", ("row", "col"), None), P("sib", None, None)),
        check_vma=False,
    )
```

time: 120 us -> 115 us (0.958)
  Pallas kernels: 54.2 us -> 66 us
  starting transfers between devices: 38.2 us -> 30.1 us
  waiting for transfers between devices: 20.3 us -> 15 us
  local copies, waits for them, and re-layouts: 4.75 us -> 0.82 us
    pallas_call x2 -> x3, Pallas kernels: 34.1 us -> 44.8 us  [strips_call(): pl.pallas_call(functools.partial(kernel, at), in_specs=[smem, hbm, vmem]...]
    ppermute x13, waiting for transfers between devices: 15.3 us -> 6.11 us  [partner(): return lax.ppermute(value, 'col', [(i, i ^ bit) for i in range(4)])]
    ppermute x13, starting transfers between devices: 23.9 us -> 17.9 us  [partner(): return lax.ppermute(value, 'col', [(i, i ^ bit) for i in range(4)])]
    ppermute x6, waiting for transfers between devices: 4.99 us -> 8.86 us  [shifted(): return lax.ppermute(value, 'row', [(i, (i + by) % n) for i in range(n)])]
    dynamic_slice x2 -> x0, local copies, waits for them, and re-layouts: 2.76 us -> none  [the longest x1 2.74 us: half_of(): return lax.dynamic_slice_in_dim(own, which * half, half, 0)]
    pallas_call x2 -> x4, Pallas kernels: 6.66 us -> 9.05 us  [the longest x1 4.95 us: diag_product(): pl.pallas_call(functools.partial(diag_kernel, at, len(pieces)), in_specs=...]
    ppermute x6, starting transfers between devices: 14.4 us -> 12.2 us  [shifted(): return lax.ppermute(value, 'row', [(i, (i + by) % n) for i in range(n)])]
  transfers between devices with their start and end apart: 19 -> 19, of which waited for: 9 -> 7; matrix products, arithmetic and copies ran while one was open for 1% -> 1% of each run, Pallas kernels for 38% -> 47%
where the time goes in v2:
time: 115 us; the launch traced here: 114 us
  Pallas kernels  66 us (57%)
  starting transfers between devices  30.1 us (26%)
  waiting for transfers between devices  15 us (13%)
  other arithmetic  1.42 us (1%)
    pallas_call x3, Pallas kernels, strips_call(): pl.pallas_call(functools.partial(kernel, at), in_specs=[smem, hbm, vmem]...  44.8 us
    ppermute x13, starting transfers between devices, partner(): return lax.ppermute(value, 'col', [(i, i ^ bit) for i in range(4)])  17.9 us
    ppermute x6, starting transfers between devices, shifted(): return lax.ppermute(value, 'row', [(i, (i + by) % n) for i in range(n)])  12.2 us
    ppermute x6, waiting for transfers between devices, shifted(): return lax.ppermute(value, 'row', [(i, (i + by) % n) for i in range(n)])  8.86 us
    ppermute x13, waiting for transfers between devices, partner(): return lax.ppermute(value, 'col', [(i, i ^ bit) for i in range(4)])  6.11 us
    pallas_call x1, Pallas kernels, diag_product(): pl.pallas_call(functools.partial(diag_kernel, at, len(pieces)), in_specs=...  4.95 us
    pallas_call x1, Pallas kernels, last_sum(): pl.pallas_call(functools.partial(last_kernel, at), grid_spec=pltpu.Prefet...  3.88 us
    pallas_call x1, Pallas kernels, last_strips(): pl.pallas_call(functools.partial(last_strips_kernel, at, len(pieces)), in...  3.47 us
  transfers between devices with their start and end apart: 19, of which 7 were waited for; matrix products, arithmetic and copies ran while one was open for 1% of the time, Pallas kernels for 47%

profile of v2, /device:TPU:0, one launch (start us, length us, event | category | flops | bytes accessed | tf_op | source)
XLA Modules:
  0.0 114.1 jit_solution(56418885887189350)
XLA Ops:
  0.6 1.4 %halves.1 = (bf16[1536,256]{1,0:T(8,128)(2,1)S(1)}, bf16[1536,256]{1,0:T(8,128)(2,1)S(1)}) custom-call(s32[1]{0:T(128)} %bitcast.7.which, bf16[3072,256]{1,0:T(8,128)(2,1)} %bitcast.19), custom_call_target="tpu_custom_call" | custom-call | flops 1000 | bytes 1000 | tf_op jit(solution)/shard_map/halves/pallas_call | solution.py:129
  2.0 3.0 %collective-permute-start = (bf16[1536,256]{1,0:T(8,128)(2,1)S(1)}, bf16[1536,256]{1,0:T(8,128)(2,1)S(1)}, u32[]{:S(2)}, u32[]{:S(2)}) collective-permute-start(bf16[1536,256]{1,0:T(8,128)(2,1)S(1)} %get-tuple-element.22.refs_1_), channel_id=1, source_target_pairs={{0,1},{1,0},{2,3},{3,2},{4,5},{5,4},{6,7},{7,6},{8,9},{9,8},{10,11... | collective-permute-start | bytes 2359304 | tf_op jit(solution)/shard_map/ppermute | solution.py:669
  5.0 0.1 pad_add_fusion
  5.1 1.2 %convert_reduce_fusion.before = s32[50]{0:T(128)S(1)} fusion(s32[12288]{0:T(1024)} %bitcast.11, s32[50]{0:T(128)S(1)} %pad_add_fusion), kind=kLoop, calls=%fused_computation | loop fusion | flops 1843150 | bytes 49552 | tf_op jit(solution)/shard_map/reduce_sum | solution.py:689
  6.4 0.1 pad_add_fusion.1.place
  6.4 1.5 %collective-permute-start.1 = (bf16[1536,256]{1,0:T(8,128)(2,1)S(1)}, bf16[1536,256]{1,0:T(8,128)(2,1)S(1)}, u32[]{:S(2)}, u32[]{:S(2)}) collective-permute-start(bf16[1536,256]{1,0:T(8,128)(2,1)S(1)} %get-tuple-element.23.refs_0_), channel_id=1, source_target_pairs={{0,2},{1,3},{2,0},{3,1},{4,6},{5,7},{6,4},{7,5},{8,10},{9,11},{10,... | collective-permute-start | bytes 2359304 | tf_op jit(solution)/shard_map/ppermute | solution.py:669
  8.0 2.2 %plan.1.refs_0_ = s32[128]{0:T(128)S(1)} custom-call(s32[50]{0:T(128)S(1)} %convert_reduce_fusion.before, s32[4]{0:T(128)S(1)} %pad_add_fusion.1.place), custom_call_target="tpu_custom_call" | custom-call | flops 1000 | bytes 1000 | tf_op jit(solution)/shard_map/plan/pallas_call | solution.py:103
  10.2 0.0 copy-start.4
  10.2 0.8 copy-done.4
  11.0 13.0 %strips_0.1.refs_6_ = f32[6144,256]{1,0:T(8,128)} custom-call(s32[128]{0:T(128)S(1)} %plan.1.refs_0_, bf16[6144,6144]{1,0:T(8,128)(2,1)} %refs_1_.5, s32[96,1,128]{2,1,0:T(1,128)S(1)} %bitcast.12, bf16[3072,256]{1,0:T(8,128)(2,1)} %bitcast.20), custom_call_target="tpu_custom_call" | custom-call | flops 19327352832 | bytes 75497472 | tf_op jit(solution)/shard_map/strips_0/pallas_call | solution.py:312
  24.0 0.0 copy-start.5
  24.0 0.0 collective-permute-done.refs_2_.refs_4_.refs_5_
  24.0 1.4 %collective-permute-done.1.refs_3_.refs_5_.refs_6_ = bf16[1536,256]{1,0:T(8,128)(2,1)S(1)} collective-permute-done((bf16[1536,256]{1,0:T(8,128)(2,1)S(1)}, bf16[1536,256]{1,0:T(8,128)(2,1)S(1)}, u32[]{:S(2)}, u32[]{:S(2)}) %collective-permute-start.1) | collective-permute-done | bytes 786464 | tf_op jit(solution)/shard_map/ppermute | solution.py:669
  25.5 1.4 %gated.1 = (bf16[1536,256]{1,0:T(8,128)(2,1)}, bf16[1536,256]{1,0:T(8,128)(2,1)}, bf16[1536,256]{1,0:T(8,128)(2,1)S(1)}, bf16[1536,256]{1,0:T(8,128)(2,1)S(1)}) custom-call(bf16[1536,256]{1,0:T(8,128)(2,1)S(1)} %get-tuple-element.23.refs_0_, bf16[1536,256]{1,0:T(8,128)(2,1)S(1)} %get-tuple-element.22.refs_1_, ...), custom_call_target="tpu_custom_call" | custom-call | flops 1000 | bytes 1000 | tf_op jit(solution)/shard_map/gated/pallas_call | solution.py:583
  26.9 1.6 %collective-permute-start.2 = (bf16[1536,256]{1,0:T(8,128)(2,1)S(1)}, bf16[1536,256]{1,0:T(8,128)(2,1)S(1)}, u32[]{:S(2)}, u32[]{:S(2)}) collective-permute-start(bf16[1536,256]{1,0:T(8,128)(2,1)S(1)} %get-tuple-element.24), channel_id=1, source_target_pairs={{0,2},{1,3},{2,0},{3,1},{4,6},{5,7},{6,4},{7,5},{8,10},{9,11},{10,... | collective-permute-start | bytes 2359304 | tf_op jit(solution)/shard_map/ppermute | solution.py:669
  28.5 0.5 collective-permute-start.3
  29.0 1.5 %collective-permute-start.4 = (bf16[1536,256]{1,0:T(8,128)(2,1)}, bf16[1536,256]{1,0:T(8,128)(2,1)}, u32[]{:S(2)}, u32[]{:S(2)}) collective-permute-start(bf16[1536,256]{1,0:T(8,128)(2,1)} %get-tuple-element.26), channel_id=1, source_target_pairs={{0,1},{1,0},{2,3},{3,2},{4,5},{5,4},{6,7},{7,6},{8,9},{9,8},{10,11... | collective-permute-start | bytes 2359304 | tf_op jit(solution)/shard_map/ppermute | solution.py:669
  30.5 0.5 collective-permute-start.5
  31.0 31.1 %strips_1.1 = (f32[6144,256]{1,0:T(8,128)S(1)}, bf16[6144,256]{1,0:T(8,128)(2,1)}) custom-call(s32[128]{0:T(128)S(1)} %plan.1.refs_0_, bf16[6144,6144]{1,0:T(8,128)(2,1)} %refs_1_.5, s32[96,1,128]{2,1,0:T(1,128)S(1)} %bitcast.13, bf16[3072,256]{1,0:T(8,128)(2,1)} %bitcast.21, bf16[1536,256]{1,0:T(8,128)(2,1)S(1)} %collective-permute-done.refs_2_.refs_4_.refs_5_, ...), custom_call_target="tpu_custom_call" | custom-call | flops 77309411328 | bytes 301989888 | tf_op jit(solution)/shard_map/strips_1/pallas_call | solution.py:312
  62.1 0.0 collective-permute-done.2.refs_6_.refs_7_
  62.2 0.7 strips_2.1
  62.8 0.4 collective-permute-done.4.refs_8_.refs_9_
  63.3 0.0 collective-permute-done.5.refs_9_.refs_10_
  63.3 3.5 %last_strips.1 = (f32[6144,256]{1,0:T(8,128)S(1)}, s16[1568,256]{1,0:T(8,128)(2,1)S(1)}, s16[1568,256]{1,0:T(8,128)(2,1)S(1)}, f32[6144,256]{1,0:T(8,128)}) custom-call(s32[128]{0:T(128)S(1)} %plan.1.refs_0_, bf16[6144,6144]{1,0:T(8,128)(2,1)} %refs_1_.5, s32[96,1,128]{2,1,0:T(1,128)S(1)} %bitcast.15, ...), custom_call_target="tpu_custom_call", output_to_operand_aliasing={{0}: (10, {})} | custom-call | flops 1000 | bytes 1000 | tf_op jit(solution)/shard_map/last_strips/pallas_call | solution.py:414
  66.8 0.6 collective-permute-start.6
  67.4 0.6 collective-permute-start.7
  68.0 4.9 %diag_product.1 = (f32[64,256]{1,0:T(8,128)S(1)}, f32[64,256]{1,0:T(8,128)S(1)}, f32[64,256]{1,0:T(8,128)S(1)}, f32[64,256]{1,0:T(8,128)S(1)}) custom-call(s32[128]{0:T(128)S(1)} %plan.1.refs_0_, f32[6144,256]{1,0:T(8,128)} %get-tuple-element.31.refs_1_.low_ref.high_ref, bf16[6144,256]{1,0:T(8,128)(2,1)} %get-tuple-element.34.refs_2_, ...), custom_call_target="tpu_custom_call" | custom-call | flops 1000 | bytes 1000 | tf_op jit(solution)/shard_map/diag_product/pallas_call | solution.py:518
  72.9 7.0 %collective-permute-start.8 = (f32[64,256]{1,0:T(8,128)S(1)}, f32[64,256]{1,0:T(8,128)S(1)}, u32[]{:S(2)}, u32[]{:S(2)}) collective-permute-start(f32[64,256]{1,0:T(8,128)S(1)} %get-tuple-element.36), channel_id=1, source_target_pairs={{0,4},{4,8},{8,12},{12,0},{1,5},{5,9},{9,13},{13,1},{2,6},{6,10},{... | collective-permute-start | bytes 196616 | tf_op jit(solution)/shard_map/ppermute | solution.py:673
  79.9 0.2 collective-permute-start.9
  80.2 2.2 %collective-permute-start.10 = (f32[64,256]{1,0:T(8,128)S(1)}, f32[64,256]{1,0:T(8,128)S(1)}, u32[]{:S(2)}, u32[]{:S(2)}) collective-permute-start(f32[64,256]{1,0:T(8,128)S(1)} %get-tuple-element.38), channel_id=1, source_target_pairs={{0,12},{4,0},{8,4},{12,8},{1,13},{5,1},{9,5},{13,9},{2,14},{6,2},{... | collective-permute-start | bytes 196616 | tf_op jit(solution)/shard_map/ppermute | solution.py:673
  82.4 2.9 %collective-permute-done.9 = f32[64,256]{1,0:T(8,128)S(1)} collective-permute-done((f32[64,256]{1,0:T(8,128)S(1)}, f32[64,256]{1,0:T(8,128)S(1)}, u32[]{:S(2)}, u32[]{:S(2)}) %collective-permute-start.9) | collective-permute-done | bytes 65568 | tf_op jit(solution)/shard_map/ppermute | solution.py:673
  85.3 0.0 copy-start.6
  85.4 3.1 %collective-permute-start.13 = (f32[64,256]{1,0:T(8,128)S(1)}, f32[64,256]{1,0:T(8,128)S(1)}, u32[]{:S(2)}, u32[]{:S(2)}) collective-permute-start(f32[64,256]{1,0:T(8,128)S(1)} %add_add_fusion.refs_0_), channel_id=1, source_target_pairs={{0,3},{1,2},{2,1},{3,0},{4,7},{5,6},{6,5},{7,4},{8,11},{9,10},{10,... | collective-permute-start | bytes 196616 | tf_op jit(solution)/shard_map/ppermute | solution.py:669
  88.4 3.6 %collective-permute-start.12 = (f32[64,256]{1,0:T(8,128)S(1)}, f32[64,256]{1,0:T(8,128)S(1)}, u32[]{:S(2)}, u32[]{:S(2)}) collective-permute-start(f32[64,256]{1,0:T(8,128)S(1)} %add_add_fusion.refs_0_), channel_id=1, source_target_pairs={{0,2},{1,3},{2,0},{3,1},{4,6},{5,7},{6,4},{7,5},{8,10},{9,11},{10,... | collective-permute-start | bytes 196616 | tf_op jit(solution)/shard_map/ppermute | solution.py:669
  92.1 2.4 %collective-permute-done.12.refs_2_ = f32[64,256]{1,0:T(8,128)S(1)} collective-permute-done((f32[64,256]{1,0:T(8,128)S(1)}, f32[64,256]{1,0:T(8,128)S(1)}, u32[]{:S(2)}, u32[]{:S(2)}) %collective-permute-start.12) | collective-permute-done | bytes 65568 | tf_op jit(solution)/shard_map/ppermute | solution.py:669
  94.4 1.9 %collective-permute-done.11.refs_1_ = f32[64,256]{1,0:T(8,128)S(1)} collective-permute-done((f32[64,256]{1,0:T(8,128)S(1)}, f32[64,256]{1,0:T(8,128)S(1)}, u32[]{:S(2)}, u32[]{:S(2)}) %collective-permute-start.11) | collective-permute-done | bytes 65568 | tf_op jit(solution)/shard_map/ppermute | solution.py:669
  96.3 0.0 collective-permute-done.6.x_in
  96.3 0.0 collective-permute-done.7.y_in
  96.3 2.6 %second_hop.1 = (s16[784,256]{1,0:T(8,128)(2,1)S(1)}, s16[784,256]{1,0:T(8,128)(2,1)S(1)}, f32[64,256]{1,0:T(8,128)S(1)}) custom-call(s32[128]{0:T(128)S(1)} %plan.1.refs_0_, f32[6144,256]{1,0:T(8,128)} %get-tuple-element.31.refs_1_.low_ref.high_ref, f32[6144,256]{1,0:T(8,128)} %get-tuple-element.31.refs_1_.low_ref.high_ref, ...), custom_call_target="tpu_custom_call" | custom-call | flops 1000 | bytes 1000 | tf_op jit(solution)/shard_map/second_hop/pallas_call | solution.py:550
  99.0 0.1 collective-permute-start.14
  99.1 1.3 %collective-permute-start.15 = (s16[784,256]{1,0:T(8,128)(2,1)S(1)}, s16[784,256]{1,0:T(8,128)(2,1)S(1)}, u32[]{:S(2)}, u32[]{:S(2)}) collective-permute-start(s16[784,256]{1,0:T(8,128)(2,1)S(1)} %get-tuple-element.40), channel_id=1, source_target_pairs={{0,1},{1,0},{2,3},{3,2},{4,5},{5,4},{6,7},{7,6},{8,9},{9,8},{10,11... | collective-permute-start | bytes 1204232 | tf_op jit(solution)/shard_map/ppermute | solution.py:669
  100.3 2.2 %collective-permute-start.18 = (f32[64,256]{1,0:T(8,128)S(1)}, f32[64,256]{1,0:T(8,128)S(1)}, u32[]{:S(2)}, u32[]{:S(2)}) collective-permute-start(f32[64,256]{1,0:T(8,128)S(1)} %get-tuple-element.41.refs_0_), channel_id=1, source_target_pairs={{0,12},{4,0},{8,4},{12,8},{1,13},{5,1},{9,5},{13,9},{2,14},{6,2},{... | collective-permute-start | bytes 196616 | tf_op jit(solution)/shard_map/ppermute | solution.py:673
  102.5 0.0 collective-permute-start.17
  102.5 0.6 collective-permute-start.16
  103.1 1.9 %collective-permute-done.18.refs_3_ = f32[64,256]{1,0:T(8,128)S(1)} collective-permute-done((f32[64,256]{1,0:T(8,128)S(1)}, f32[64,256]{1,0:T(8,128)S(1)}, u32[]{:S(2)}, u32[]{:S(2)}) %collective-permute-start.18) | collective-permute-done | bytes 65568 | tf_op jit(solution)/shard_map/ppermute | solution.py:673
  105.0 4.0 %collective-permute-done.17.refs_2_ = f32[64,256]{1,0:T(8,128)S(1)} collective-permute-done((f32[64,256]{1,0:T(8,128)S(1)}, f32[64,256]{1,0:T(8,128)S(1)}, u32[]{:S(2)}, u32[]{:S(2)}) %collective-permute-start.17) | collective-permute-done | bytes 65568 | tf_op jit(solution)/shard_map/ppermute | solution.py:673
  109.0 1.3 %together.1 = f32[256,256]{1,0:T(8,128)} custom-call(s32[128]{0:T(128)S(1)} %plan.1.refs_0_, f32[256,256]{1,0:T(8,128)S(1)} %bitcast.18, f32[64,256]{1,0:T(8,128)S(1)} %get-tuple-element.41.refs_0_, f32[64,256]{1,0:T(8,128)S(1)} %collective-permute-done.16.refs_1_, f32[64,256]{1,0:T(8,128)S(1)} %collective-permute-done.17.refs_2_, ...), custom_call_target="tpu_custom_call" | custom-call | flops 1000 | bytes 1000 | tf_op jit(solution)/shard_map/together/pallas_call | solution.py:647
  110.3 3.9 %last_sum.1 = f32[1536,256]{1,0:T(8,128)} custom-call(s32[128]{0:T(128)S(1)} %plan.1.refs_0_, f32[6144,256]{1,0:T(8,128)} %get-tuple-element.31.refs_1_.low_ref.high_ref, f32[6144,256]{1,0:T(8,128)} %get-tuple-element.31.refs_1_.low_ref.high_ref, s16[1568,256]{1,0:T(8,128)(2,1)S(1)} %collective-permute-done.6.x_in, ...), custom_call_target="tpu_custom_call" | custom-call | flops 1000 | bytes 1000 | tf_op jit(solution)/shard_map/last_sum/pallas_call | solution.py:617
  (20 shorter events, 0.1 us)
Async XLA Ops:
  2.0 22.0 %collective-permute-start = (bf16[1536,256]{1,0:T(8,128)(2,1)S(1)}, bf16[1536,256]{1,0:T(8,128)(2,1)S(1)}, u32[]{:S(2)}, u32[]{:S(2)}) collective-permute-start(bf16[1536,256]{1,0:T(8,128)(2,1)S(1)} %get-tuple-element.22.refs_1_), channel_id=1, source_target_pairs={{0,1},{1,0},{2,3},{3,2},{4,5},{5,4},{6,7},{7,6},{8,9},{9,8},{10,11... | collective-permute-start | bytes 2359304 | tf_op jit(solution)/shard_map/ppermute | solution.py:669
  6.4 19.0 %collective-permute-start.1 = (bf16[1536,256]{1,0:T(8,128)(2,1)S(1)}, bf16[1536,256]{1,0:T(8,128)(2,1)S(1)}, u32[]{:S(2)}, u32[]{:S(2)}) collective-permute-start(bf16[1536,256]{1,0:T(8,128)(2,1)S(1)} %get-tuple-element.23.refs_0_), channel_id=1, source_target_pairs={{0,2},{1,3},{2,0},{3,1},{4,6},{5,7},{6,4},{7,5},{8,10},{9,11},{10,... | collective-permute-start | bytes 2359304 | tf_op jit(solution)/shard_map/ppermute | solution.py:669
  10.2 0.8 copy-start.4
  24.0 7.0 %copy-start.5 = (s32[1,12288]{1,0:T(1,128)S(1)}, s32[1,12288]{1,0:T(1,128)}, u32[]{:S(2)}) copy-start(s32[1,12288]{1,0:T(1,128)} %param.6) | copy-start | bytes 147460
  24.0 39.2 %copy-start = (bf16[1536,256]{1,0:T(8,128)(2,1)}, bf16[1536,256]{1,0:T(8,128)(2,1)S(1)}, u32[]{:S(2)}) copy-start(bf16[1536,256]{1,0:T(8,128)(2,1)S(1)} %collective-permute-done.refs_2_.refs_4_.refs_5_) | copy-start | bytes 2359300
  25.5 37.8 %copy-start.1 = (bf16[1536,256]{1,0:T(8,128)(2,1)}, bf16[1536,256]{1,0:T(8,128)(2,1)S(1)}, u32[]{:S(2)}) copy-start(bf16[1536,256]{1,0:T(8,128)(2,1)S(1)} %collective-permute-done.1.refs_3_.refs_5_.refs_6_) | copy-start | bytes 2359300
  26.9 35.2 %collective-permute-start.2 = (bf16[1536,256]{1,0:T(8,128)(2,1)S(1)}, bf16[1536,256]{1,0:T(8,128)(2,1)S(1)}, u32[]{:S(2)}, u32[]{:S(2)}) collective-permute-start(bf16[1536,256]{1,0:T(8,128)(2,1)S(1)} %get-tuple-element.24), channel_id=1, source_target_pairs={{0,2},{1,3},{2,0},{3,1},{4,6},{5,7},{6,4},{7,5},{8,10},{9,11},{10,... | collective-permute-start | bytes 2359304 | tf_op jit(solution)/shard_map/ppermute | solution.py:669
  28.5 33.6 %collective-permute-start.3 = (bf16[1536,256]{1,0:T(8,128)(2,1)S(1)}, bf16[1536,256]{1,0:T(8,128)(2,1)S(1)}, u32[]{:S(2)}, u32[]{:S(2)}) collective-permute-start(bf16[1536,256]{1,0:T(8,128)(2,1)S(1)} %get-tuple-element.25), channel_id=1, source_target_pairs={{0,1},{1,0},{2,3},{3,2},{4,5},{5,4},{6,7},{7,6},{8,9},{9,8},{10,11... | collective-permute-start | bytes 2359304 | tf_op jit(solution)/shard_map/ppermute | solution.py:669
  29.0 34.2 %collective-permute-start.4 = (bf16[1536,256]{1,0:T(8,128)(2,1)}, bf16[1536,256]{1,0:T(8,128)(2,1)}, u32[]{:S(2)}, u32[]{:S(2)}) collective-permute-start(bf16[1536,256]{1,0:T(8,128)(2,1)} %get-tuple-element.26), channel_id=1, source_target_pairs={{0,1},{1,0},{2,3},{3,2},{4,5},{5,4},{6,7},{7,6},{8,9},{9,8},{10,11... | collective-permute-start | bytes 2359304 | tf_op jit(solution)/shard_map/ppermute | solution.py:669
  30.5 32.7 %collective-permute-start.5 = (bf16[1536,256]{1,0:T(8,128)(2,1)}, bf16[1536,256]{1,0:T(8,128)(2,1)}, u32[]{:S(2)}, u32[]{:S(2)}) collective-permute-start(bf16[1536,256]{1,0:T(8,128)(2,1)} %get-tuple-element.27), channel_id=1, source_target_pairs={{0,2},{1,3},{2,0},{3,1},{4,6},{5,7},{6,4},{7,5},{8,10},{9,11},{10,... | collective-permute-start | bytes 2359304 | tf_op jit(solution)/shard_map/ppermute | solution.py:669
  62.1 1.1 %copy-start.2 = (bf16[1536,256]{1,0:T(8,128)(2,1)}, bf16[1536,256]{1,0:T(8,128)(2,1)S(1)}, u32[]{:S(2)}) copy-start(bf16[1536,256]{1,0:T(8,128)(2,1)S(1)} %collective-permute-done.2.refs_6_.refs_7_) | copy-start | bytes 2359300
  62.1 1.1 copy-start.3
  66.8 29.6 %collective-permute-start.6 = (s16[1568,256]{1,0:T(8,128)(2,1)S(1)}, s16[1568,256]{1,0:T(8,128)(2,1)S(1)}, u32[]{:S(2)}, u32[]{:S(2)}) collective-permute-start(s16[1568,256]{1,0:T(8,128)(2,1)S(1)} %get-tuple-element.32), channel_id=1, source_target_pairs={{0,1},{1,0},{2,3},{3,2},{4,5},{5,4},{6,7},{7,6},{8,9},{9,8},{10,11... | collective-permute-start | bytes 2408456 | tf_op jit(solution)/shard_map/ppermute | solution.py:669
  67.4 29.0 %collective-permute-start.7 = (s16[1568,256]{1,0:T(8,128)(2,1)S(1)}, s16[1568,256]{1,0:T(8,128)(2,1)S(1)}, u32[]{:S(2)}, u32[]{:S(2)}) collective-permute-start(s16[1568,256]{1,0:T(8,128)(2,1)S(1)} %get-tuple-element.33), channel_id=1, source_target_pairs={{0,2},{1,3},{2,0},{3,1},{4,6},{5,7},{6,4},{7,5},{8,10},{9,11},{10,... | collective-permute-start | bytes 2408456 | tf_op jit(solution)/shard_map/ppermute | solution.py:669
  72.9 9.5 %collective-permute-start.8 = (f32[64,256]{1,0:T(8,128)S(1)}, f32[64,256]{1,0:T(8,128)S(1)}, u32[]{:S(2)}, u32[]{:S(2)}) collective-permute-start(f32[64,256]{1,0:T(8,128)S(1)} %get-tuple-element.36), channel_id=1, source_target_pairs={{0,4},{4,8},{8,12},{12,0},{1,5},{5,9},{9,13},{13,1},{2,6},{6,10},{... | collective-permute-start | bytes 196616 | tf_op jit(solution)/shard_map/ppermute | solution.py:673
  79.9 5.4 %collective-permute-start.9 = (f32[64,256]{1,0:T(8,128)S(1)}, f32[64,256]{1,0:T(8,128)S(1)}, u32[]{:S(2)}, u32[]{:S(2)}) collective-permute-start(f32[64,256]{1,0:T(8,128)S(1)} %get-tuple-element.37), channel_id=1, source_target_pairs={{0,8},{4,12},{8,0},{12,4},{1,9},{5,13},{9,1},{13,5},{2,10},{6,14},... | collective-permute-start | bytes 196616 | tf_op jit(solution)/shard_map/ppermute | solution.py:673
  80.2 5.1 %collective-permute-start.10 = (f32[64,256]{1,0:T(8,128)S(1)}, f32[64,256]{1,0:T(8,128)S(1)}, u32[]{:S(2)}, u32[]{:S(2)}) collective-permute-start(f32[64,256]{1,0:T(8,128)S(1)} %get-tuple-element.38), channel_id=1, source_target_pairs={{0,12},{4,0},{8,4},{12,8},{1,13},{5,1},{9,5},{13,9},{2,14},{6,2},{... | collective-permute-start | bytes 196616 | tf_op jit(solution)/shard_map/ppermute | solution.py:673
  85.3 23.6 %copy-start.6 = (f32[1,256,256]{2,1,0:T(8,128)S(1)}, f32[1,256,256]{2,1,0:T(8,128)}, u32[]{:S(2)}) copy-start(f32[1,256,256]{2,1,0:T(8,128)} %param.7) | copy-start | bytes 786436
  85.4 6.7 %collective-permute-start.13 = (f32[64,256]{1,0:T(8,128)S(1)}, f32[64,256]{1,0:T(8,128)S(1)}, u32[]{:S(2)}, u32[]{:S(2)}) collective-permute-start(f32[64,256]{1,0:T(8,128)S(1)} %add_add_fusion.refs_0_), channel_id=1, source_target_pairs={{0,3},{1,2},{2,1},{3,0},{4,7},{5,6},{6,5},{7,4},{8,11},{9,10},{10,... | collective-permute-start | bytes 196616 | tf_op jit(solution)/shard_map/ppermute | solution.py:669
  88.4 6.0 %collective-permute-start.12 = (f32[64,256]{1,0:T(8,128)S(1)}, f32[64,256]{1,0:T(8,128)S(1)}, u32[]{:S(2)}, u32[]{:S(2)}) collective-permute-start(f32[64,256]{1,0:T(8,128)S(1)} %add_add_fusion.refs_0_), channel_id=1, source_target_pairs={{0,2},{1,3},{2,0},{3,1},{4,6},{5,7},{6,4},{7,5},{8,10},{9,11},{10,... | collective-permute-start | bytes 196616 | tf_op jit(solution)/shard_map/ppermute | solution.py:669
  92.1 4.3 %collective-permute-start.11 = (f32[64,256]{1,0:T(8,128)S(1)}, f32[64,256]{1,0:T(8,128)S(1)}, u32[]{:S(2)}, u32[]{:S(2)}) collective-permute-start(f32[64,256]{1,0:T(8,128)S(1)} %add_add_fusion.refs_0_), channel_id=1, source_target_pairs={{0,1},{1,0},{2,3},{3,2},{4,5},{5,4},{6,7},{7,6},{8,9},{9,8},{10,11... | collective-permute-start | bytes 196616 | tf_op jit(solution)/shard_map/ppermute | solution.py:669
  99.0 11.3 %collective-permute-start.14 = (s16[784,256]{1,0:T(8,128)(2,1)S(1)}, s16[784,256]{1,0:T(8,128)(2,1)S(1)}, u32[]{:S(2)}, u32[]{:S(2)}) collective-permute-start(s16[784,256]{1,0:T(8,128)(2,1)S(1)} %get-tuple-element.39), channel_id=1, source_target_pairs={{0,2},{1,3},{2,0},{3,1},{4,6},{5,7},{6,4},{7,5},{8,10},{9,11},{10,... | collective-permute-start | bytes 1204232 | tf_op jit(solution)/shard_map/ppermute | solution.py:669
  99.1 11.2 %collective-permute-start.15 = (s16[784,256]{1,0:T(8,128)(2,1)S(1)}, s16[784,256]{1,0:T(8,128)(2,1)S(1)}, u32[]{:S(2)}, u32[]{:S(2)}) collective-permute-start(s16[784,256]{1,0:T(8,128)(2,1)S(1)} %get-tuple-element.40), channel_id=1, source_target_pairs={{0,1},{1,0},{2,3},{3,2},{4,5},{5,4},{6,7},{7,6},{8,9},{9,8},{10,11... | collective-permute-start | bytes 1204232 | tf_op jit(solution)/shard_map/ppermute | solution.py:669
  100.3 4.7 %collective-permute-start.18 = (f32[64,256]{1,0:T(8,128)S(1)}, f32[64,256]{1,0:T(8,128)S(1)}, u32[]{:S(2)}, u32[]{:S(2)}) collective-permute-start(f32[64,256]{1,0:T(8,128)S(1)} %get-tuple-element.41.refs_0_), channel_id=1, source_target_pairs={{0,12},{4,0},{8,4},{12,8},{1,13},{5,1},{9,5},{13,9},{2,14},{6,2},{... | collective-permute-start | bytes 196616 | tf_op jit(solution)/shard_map/ppermute | solution.py:673
  102.5 6.5 %collective-permute-start.17 = (f32[64,256]{1,0:T(8,128)S(1)}, f32[64,256]{1,0:T(8,128)S(1)}, u32[]{:S(2)}, u32[]{:S(2)}) collective-permute-start(f32[64,256]{1,0:T(8,128)S(1)} %get-tuple-element.41.refs_0_), channel_id=1, source_target_pairs={{0,8},{4,12},{8,0},{12,4},{1,9},{5,13},{9,1},{13,5},{2,10},{6,14},... | collective-permute-start | bytes 196616 | tf_op jit(solution)/shard_map/ppermute | solution.py:673
  102.5 6.5 %collective-permute-start.16 = (f32[64,256]{1,0:T(8,128)S(1)}, f32[64,256]{1,0:T(8,128)S(1)}, u32[]{:S(2)}, u32[]{:S(2)}) collective-permute-start(f32[64,256]{1,0:T(8,128)S(1)} %get-tuple-element.41.refs_0_), channel_id=1, source_target_pairs={{0,4},{4,8},{8,12},{12,0},{1,5},{5,9},{9,13},{13,1},{2,6},{6,10},{... | collective-permute-start | bytes 196616 | tf_op jit(solution)/shard_map/ppermute | solution.py:673
